TPU v7x, 512 devices: a whole 4x4x16 slice. The times are simulated.
512 devices in a mesh: section: 8 (over z_hi, core), pool: 64 (over x, y, z_lo).
Axes of the slice: x: 4, y: 4, z: 16 (z_hi: 4, z_lo: 4; z = z_hi * 4 + z_lo), core: 2. Of those that a mesh axis runs over, the one named last changes fastest.
Arguments:
- activations: bfloat16 [8, 64, 16, 8, 5120], P('section', 'pool'), may hold values from -6 to 6
- cotangents: bfloat16 [8, 64, 16, 8, 5120], P('section', 'pool'), may hold values from -6 to 6
- token_counts: int32 [8, 64, 16], P('section', 'pool'), may hold values from 0 to 8, as said below
- route_ahead: int32 [8, 64, 16], P('section', 'pool'), may hold values from 0 to 63, as said below
- route_back: int32 [8, 64, 16], P('section', 'pool'), may hold values from 0 to 63, as said below
- down_rows: bfloat16 [8, 64, 5120], P('section', 'pool'), may hold values from -0.078125 to 0.078125
- up_rows: bfloat16 [8, 64, 5120], P('section', 'pool'), may hold values from -0.75 to 0.75
- norm_gain: bfloat16 [8, 5120], P('section'), may hold values from 0.099609375 to 1.8984375
Outputs:
- arrived_ahead: bfloat16 [8, 64, 12, 8, 5120], P('section', 'pool')
- arrived_back: bfloat16 [8, 64, 12, 8, 5120], P('section', 'pool')
- grad_down: float32 [8, 64, 5120], P('section', 'pool')
- grad_up: float32 [8, 64, 5120], P('section', 'pool')
Inputs may be any that keep to these rules, and one draw needn't show every extreme that they name: `token_counts`: A device's live micro-batches fill its first slots, at most 12 of them, with 1 to 8 tokens each, and the later slots hold 0; the first slot of every device holds 8 tokens. `route_ahead`: the live slots of one device name distinct receivers. In every section no receiver is named by more than 12 live slots of the section's pool, and one receiver by exactly 12. Entries of empty slots are arbitrary. `route_back`: the live slots of one device name distinct devices. In every section no device is named by more than 12 live slots of the section's pool, and one by exactly 12. Entries of empty slots are arbitrary.
All inputs are finite; a program needn't handle non-finite values.
Results may differ from a plain program's by a relative error of at most 0.0053.
Values may be sent and summed in bfloat16 or wider, within the bound.
A program may use at most 128 MiB of HBM per device.

v0:
```python
import jax
import jax.numpy as jnp
from jax import lax
from jax.sharding import PartitionSpec as P

CAP = 12


epsilon = 1e-05


def from_behind(value, axis, steps):
    count = lax.axis_size(axis)
    first, last = (max(0, -steps), min(count, count - steps))
    return lax.ppermute(value, axis, [(source, source + steps) for source in range(first, last)])


def adapter_pass(section_in, grad_in, sizes, down_full, up_full, gain_row):
    slot_count, depth, width = section_in.shape
    row_ids = jnp.arange(depth, dtype=jnp.int32)
    keep_rows = (row_ids[None, :] < sizes[:, None]).reshape(slot_count * depth, 1)
    wide_in = section_in.reshape(slot_count * depth, width).astype(jnp.float32)
    gain_wide = gain_row.astype(jnp.float32)
    inv_rms = lax.rsqrt(jnp.mean(wide_in * wide_in, axis=1, keepdims=True) + epsilon)
    normed = (wide_in * inv_rms * gain_wide).astype(jnp.bfloat16)
    preact = lax.dot_general(
        normed, down_full, (((1,), (1,)), ((), ())), preferred_element_type=jnp.float32
    )
    gates = jax.nn.sigmoid(preact)
    hidden = (preact * gates).astype(jnp.bfloat16)
    branch = jnp.dot(hidden, up_full, preferred_element_type=jnp.float32)
    outward = jnp.where(keep_rows, wide_in + branch, 0.0).astype(jnp.bfloat16)
    grad_out = jnp.where(
        keep_rows, grad_in.reshape(slot_count * depth, width), jnp.zeros((), grad_in.dtype)
    )
    grad_up = lax.dot_general(
        hidden, grad_out, (((0,), (0,)), ((), ())), preferred_element_type=jnp.float32
    )
    back_sum = lax.dot_general(
        grad_out, up_full, (((1,), (1,)), ((), ())), preferred_element_type=jnp.float32
    )
    slope_term = (back_sum * gates * (1.0 + preact * (1.0 - gates))).astype(jnp.bfloat16)
    grad_down = lax.dot_general(
        slope_term, normed, (((0,), (0,)), ((), ())), preferred_element_type=jnp.float32
    )
    through = jnp.dot(slope_term, down_full, preferred_element_type=jnp.float32) * gain_wide
    centred = jnp.mean(through * wide_in, axis=1, keepdims=True)
    inward = (
        grad_out.astype(jnp.float32) + inv_rms * (through - wide_in * inv_rms * inv_rms * centred)
    ).astype(jnp.bfloat16)
    return (outward.reshape(section_in.shape), inward.reshape(section_in.shape), grad_down, grad_up)


def spread(values, sizes, targets, peer_count):
    slot_ids = jnp.arange(values.shape[0], dtype=jnp.int32)
    peer_ids = jnp.arange(peer_count, dtype=jnp.int32)
    hits = ((targets[None, :] == peer_ids[:, None]) & (sizes[None, :] > 0)).astype(jnp.int32)
    which_slot = jnp.sum(hits * slot_ids[None, :], axis=1)
    has_item = jnp.sum(hits, axis=1) > 0
    buffer = jnp.where(has_item[:, None, None], values[which_slot], jnp.zeros((), values.dtype))
    marks = jnp.where(has_item, sizes[which_slot], 0).astype(jnp.bfloat16)
    return (buffer, marks)


def collect(buffer, marks, slot_count):
    arrived = (marks > 0).astype(jnp.int32)
    position = jnp.cumsum(arrived) - 1
    peer_ids = jnp.arange(buffer.shape[0], dtype=jnp.int32)
    slot_ids = jnp.arange(slot_count, dtype=jnp.int32)
    matched = (position[None, :] == slot_ids[:, None]) & (arrived[None, :] > 0)
    source = jnp.sum(matched.astype(jnp.int32) * peer_ids[None, :], axis=1)
    valid_slot = jnp.any(matched, axis=1)
    return jnp.where(valid_slot[:, None, None], buffer[source], jnp.zeros((), buffer.dtype))


def shards(
    activations, cotangents, token_counts, route_ahead, route_back, down_rows, up_rows, norm_gain
):
    section_in = activations[0, 0]
    grad_in = cotangents[0, 0]
    sizes = token_counts[0, 0]
    ahead_to = route_ahead[0, 0]
    back_to = route_back[0, 0]
    down_full, up_full = (
        lax.all_gather(down_rows[0], "pool", axis=0, tiled=True),
        lax.all_gather(up_rows[0], "pool", axis=0, tiled=True),
    )
    outward, inward, grad_down, grad_up = adapter_pass(
        section_in, grad_in, sizes, down_full, up_full, norm_gain[0]
    )
    peer_count = lax.axis_size("pool")
    carried = from_behind(
        (outward, sizes.astype(jnp.bfloat16), ahead_to.astype(jnp.bfloat16)), "section", 1
    )
    ahead_buf, ahead_marks = spread(
        carried[0], carried[1].astype(jnp.int32), carried[2].astype(jnp.int32), peer_count
    )
    ahead_buf, ahead_marks = (
        lax.all_to_all(ahead_buf, "pool", split_axis=0, concat_axis=0, tiled=True),
        lax.all_to_all(ahead_marks, "pool", split_axis=0, concat_axis=0, tiled=True),
    )
    forward_in = collect(ahead_buf, ahead_marks, CAP)
    returned = from_behind(
        (inward, sizes.astype(jnp.bfloat16), back_to.astype(jnp.bfloat16)), "section", -1
    )
    back_buf, back_marks = spread(
        returned[0], returned[1].astype(jnp.int32), returned[2].astype(jnp.int32), peer_count
    )
    back_buf, back_marks = (
        lax.all_to_all(back_buf, "pool", split_axis=0, concat_axis=0, tiled=True),
        lax.all_to_all(back_marks, "pool", split_axis=0, concat_axis=0, tiled=True),
    )
    behind = collect(back_buf, back_marks, CAP)
    share_down, share_up = (
        lax.psum_scatter(grad_down, "pool", scatter_dimension=0, tiled=True),
        lax.psum_scatter(grad_up, "pool", scatter_dimension=0, tiled=True),
    )
    return (forward_in[None, None], behind[None, None], share_down[None], share_up[None])


def solution(mesh):
    placed = (
        P("section", "pool", None, None, None),
        P("section", "pool", None, None, None),
        P("section", "pool", None),
        P("section", "pool", None),
        P("section", "pool", None),
        P("section", "pool", None),
        P("section", "pool", None),
        P("section", None),
    )
    return jax.shard_map(
        shards,
        mesh=mesh,
        in_specs=placed,
        out_specs=(
            P("section", "pool", None, None, None),
            P("section", "pool", None, None, None),
            P("section", "pool", None),
            P("section", "pool", None),
        ),
        check_vma=False,
    )
```

profile of v0, /device:TPU:128, one launch (start us, length us, event | category | flops | bytes accessed | tf_op | source)
XLA Modules:
  0.0 1452.3 jit_solution(7379644592585838274)
XLA Ops:
  8.0 1.9 collective-permute-start.4
  9.9 2.4 collective-permute-start.1
  12.9 7.1 collective-permute-start.3
  20.7 3.6 collective-permute-start
  25.1 1.7 fusion.14
  27.6 197.8 %all-gather = bf16[64,1,5120]{2,1,0:T(2,128)(2,1)S(1)} all-gather(bf16[1,1,5120]{2,1,0:T(2,128)(2,1)} %param.13), channel_id=2, replica_groups=mesh['section'=8,'pool'=64] {'pool'}, dimensions={0}, use_global_device_ids=true | all-gather | bytes 665600 | tf_op jit(solution)/shard_map/all_gather | solution.py:85
  225.4 190.7 %all-gather.1 = bf16[64,1,5120]{2,1,0:T(2,128)(2,1)S(1)} all-gather(bf16[1,1,5120]{2,1,0:T(2,128)(2,1)S(1)} %copy-done.6), channel_id=3, replica_groups=mesh['section'=8,'pool'=64] {'pool'}, dimensions={0}, use_global_device_ids=true | all-gather | bytes 665600 | tf_op jit(solution)/shard_map/all_gather | solution.py:86
  416.7 1.7 fusion.2
  418.4 1.9 collective-permute-start.2
  422.0 4.6 all-to-all-start
  428.3 13.2 collective-permute-done.2
  441.6 3.2 gather_fusion.1
  444.8 40.0 %all-to-all-start.2 = ((bf16[64,1,1]{2,1,0:T(2,128)(2,1)}), bf16[64,1,1]{2,1,0:T(2,128)(2,1)S(1)}, u32[]{:S(2)}, u32[]{:S(2)}) async-start(bf16[64,1,1]{2,1,0:T(2,128)(2,1)} %copy.28), calls=%async_computation.2 | async-start | bytes 65536 | tf_op jit(solution)/shard_map/all_to_all | solution.py:111
  484.8 5.2 broadcast_select_fusion.1
  490.1 4.5 all-to-all-done.2
  494.6 6.5 all-to-all-start.1
  501.1 2.1 fusion.17
  504.9 4.7 collective-permute-start.5
  509.7 15.1 %collective-permute-done.5 = bf16[16,8,5120]{2,1,0:T(8,128)(2,1)S(1)} collective-permute-done((bf16[16,8,5120]{2,1,0:T(8,128)(2,1)S(1)}, bf16[16,8,5120]{2,1,0:T(8,128)(2,1)S(1)}, u32[]{:S(2)}, u32[]{:S(2)}) %collective-permute-start.5) | collective-permute-done | bytes 1310752 | tf_op jit(solution)/shard_map/ppermute | solution.py:15
  524.8 3.3 gather_fusion.4
  528.0 5.3 broadcast_select_fusion
  533.3 129.5 %all-to-all-done.1 = bf16[64,8,5120]{2,1,0:T(8,128)(2,1)} async-done(((bf16[64,8,5120]{2,1,0:T(8,128)(2,1)}), bf16[64,8,5120]{2,1,0:T(8,128)(2,1)}, u32[]{:S(2)}, u32[]{:S(2)}) %all-to-all-start.1) | async-done | bytes 5242912 | tf_op jit(solution)/shard_map/all_to_all | solution.py:99
  662.8 27.0 %all-to-all-start.3 = ((bf16[64,8,5120]{2,1,0:T(8,128)(2,1)}), bf16[64,8,5120]{2,1,0:T(8,128)(2,1)}, u32[]{:S(2)}, u32[]{:S(2)}) async-start(bf16[64,8,5120]{2,1,0:T(8,128)(2,1)} %broadcast_select_fusion), calls=%async_computation.3 | async-start | bytes 10485760 | tf_op jit(solution)/shard_map/all_to_all | solution.py:110
  690.1 1.5 fusion.40
  691.6 1.7 fusion.23
  693.3 1.3 dynamic-slice
  694.5 1.2 compare_reduce_fusion.1
  695.9 1.2 compare_reduce_fusion
  698.0 736.9 %all-reduce.5.cloned.1.call-done = (f32[64,5120]{1,0:T(8,128)}, f32[64,5120]{1,0:T(8,128)}) async-done(((f32[64,5120]{1,0:T(8,128)}, f32[64,5120]{1,0:T(8,128)}), (f32[64,5120]{1,0:T(8,128)}, f32[64,5120]{1,0:T(8,128)})) %all-reduce.5.cloned.1.call-update) | async-done | bytes 2621456
  1434.8 2.3 dynamic-slice_bitcast_fusion
  1437.1 3.1 gather_fusion.2
  1441.3 3.1 gather_fusion.5
  (68 shorter events, 12.8 us)
Async XLA Ops:
  7.2 408.9 %copy-start = (bf16[1,1,16,8,5120]{4,3,2,1,0:T(8,128)(2,1)S(1)}, bf16[1,1,16,8,5120]{4,3,2,1,0:T(8,128)(2,1)}, u32[]{:S(2)}) copy-start(bf16[1,1,16,8,5120]{4,3,2,1,0:T(8,128)(2,1)} %param.8) | copy-start | bytes 3932164
  7.2 218.2 %copy-start.6 = (bf16[1,1,5120]{2,1,0:T(2,128)(2,1)S(1)}, bf16[1,1,5120]{2,1,0:T(2,128)(2,1)}, u32[]{:S(2)}) copy-start(bf16[1,1,5120]{2,1,0:T(2,128)(2,1)} %param.14) | copy-start | bytes 30724
  8.0 418.7 %collective-permute-start.4 = (bf16[16]{0:T(256)(128)(2,1)S(1)}, bf16[16]{0:T(256)(128)(2,1)S(1)}, u32[]{:S(2)}, u32[]{:S(2)}) collective-permute-start(bf16[16]{0:T(256)(128)(2,1)S(1)} %bitcast_convert_fusion), channel_id=1, source_target_pairs={{64,0},{128,64},{192,128},{256,192},{320,256},{384,320},{448,384},... | collective-permute-start | bytes 104 | tf_op jit(solution)/shard_map/ppermute | solution.py:15
  9.9 410.5 %collective-permute-start.1 = (bf16[16]{0:T(256)(128)(2,1)S(1)}, bf16[16]{0:T(256)(128)(2,1)S(1)}, u32[]{:S(2)}, u32[]{:S(2)}) collective-permute-start(bf16[16]{0:T(256)(128)(2,1)S(1)} %bitcast_convert_fusion), channel_id=1, source_target_pairs={{0,64},{64,128},{128,192},{192,256},{256,320},{320,384},{384,448},... | collective-permute-start | bytes 104 | tf_op jit(solution)/shard_map/ppermute | solution.py:15
  12.9 413.7 %collective-permute-start.3 = (bf16[16]{0:T(256)(128)(2,1)S(1)}, bf16[16]{0:T(256)(128)(2,1)S(1)}, u32[]{:S(2)}, u32[]{:S(2)}) collective-permute-start(bf16[16]{0:T(256)(128)(2,1)S(1)} %convert_bitcast_fusion.2), channel_id=1, source_target_pairs={{64,0},{128,64},{192,128},{256,192},{320,256},{384,320},{448,384},... | collective-permute-start | bytes 104 | tf_op jit(solution)/shard_map/ppermute | solution.py:15
  20.7 399.7 %collective-permute-start = (bf16[16]{0:T(256)(128)(2,1)S(1)}, bf16[16]{0:T(256)(128)(2,1)S(1)}, u32[]{:S(2)}, u32[]{:S(2)}) collective-permute-start(bf16[16]{0:T(256)(128)(2,1)S(1)} %convert_bitcast_fusion.4), channel_id=1, source_target_pairs={{0,64},{64,128},{128,192},{192,256},{256,320},{320,384},{384,448},... | collective-permute-start | bytes 104 | tf_op jit(solution)/shard_map/ppermute | solution.py:15
  225.4 190.7 %copy-start.4 = (bf16[64,1,5120]{2,1,0:T(2,128)(2,1)}, bf16[64,1,5120]{2,1,0:T(2,128)(2,1)S(1)}, u32[]{:S(2)}) copy-start(bf16[64,1,5120]{2,1,0:T(2,128)(2,1)S(1)} %all-gather) | copy-start | bytes 1966084
  416.0 2.4 copy-start.3
  418.4 23.1 %collective-permute-start.2 = (bf16[16,8,5120]{2,1,0:T(8,128)(2,1)}, bf16[16,8,5120]{2,1,0:T(8,128)(2,1)S(1)}, u32[]{:S(2)}, u32[]{:S(2)}) collective-permute-start(bf16[16,8,5120]{2,1,0:T(8,128)(2,1)} %fusion.2), channel_id=1, source_target_pairs={{0,64},{64,128},{128,192},{192,256},{256,320},{320,384},{384,448},... | collective-permute-start | bytes 3932168 | tf_op jit(solution)/shard_map/ppermute | solution.py:15
  422.0 22.8 %all-to-all-start = ((bf16[64,1,1]{2,1,0:T(2,128)(2,1)}), bf16[64,1,1]{2,1,0:T(2,128)(2,1)S(1)}, u32[]{:S(2)}, u32[]{:S(2)}) async-start(bf16[64,1,1]{2,1,0:T(2,128)(2,1)} %copy.26), calls=%async_computation | async-start | bytes 65536 | tf_op jit(solution)/shard_map/all_to_all | solution.py:100
  444.8 49.7 %all-to-all-start.2 = ((bf16[64,1,1]{2,1,0:T(2,128)(2,1)}), bf16[64,1,1]{2,1,0:T(2,128)(2,1)S(1)}, u32[]{:S(2)}, u32[]{:S(2)}) async-start(bf16[64,1,1]{2,1,0:T(2,128)(2,1)} %copy.28), calls=%async_computation.2 | async-start | bytes 65536 | tf_op jit(solution)/shard_map/all_to_all | solution.py:111
  490.1 11.0 copy-start.1
  494.6 168.2 %all-to-all-start.1 = ((bf16[64,8,5120]{2,1,0:T(8,128)(2,1)}), bf16[64,8,5120]{2,1,0:T(8,128)(2,1)}, u32[]{:S(2)}, u32[]{:S(2)}) async-start(bf16[64,8,5120]{2,1,0:T(8,128)(2,1)} %broadcast_select_fusion.1), calls=%async_computation.1 | async-start | bytes 10485760 | tf_op jit(solution)/shard_map/all_to_all | solution.py:99
  501.1 2.1 copy-start.5
  504.9 19.9 %collective-permute-start.5 = (bf16[16,8,5120]{2,1,0:T(8,128)(2,1)S(1)}, bf16[16,8,5120]{2,1,0:T(8,128)(2,1)S(1)}, u32[]{:S(2)}, u32[]{:S(2)}) collective-permute-start(bf16[16,8,5120]{2,1,0:T(8,128)(2,1)S(1)} %fusion.15), channel_id=1, source_target_pairs={{64,0},{128,64},{192,128},{256,192},{320,256},{384,320},{448,384},... | collective-permute-start | bytes 3932168 | tf_op jit(solution)/shard_map/ppermute | solution.py:15
  533.3 156.8 %copy-start.2 = (bf16[1,1,16,8,5120]{4,3,2,1,0:T(8,128)(2,1)S(1)}, bf16[1,1,16,8,5120]{4,3,2,1,0:T(8,128)(2,1)}, u32[]{:S(2)}) copy-start(bf16[1,1,16,8,5120]{4,3,2,1,0:T(8,128)(2,1)} %param.9) | copy-start | bytes 3932164
  662.8 778.5 %all-to-all-start.3 = ((bf16[64,8,5120]{2,1,0:T(8,128)(2,1)}), bf16[64,8,5120]{2,1,0:T(8,128)(2,1)}, u32[]{:S(2)}, u32[]{:S(2)}) async-start(bf16[64,8,5120]{2,1,0:T(8,128)(2,1)} %broadcast_select_fusion), calls=%async_computation.3 | async-start | bytes 10485760 | tf_op jit(solution)/shard_map/all_to_all | solution.py:110
  689.8 745.0 %all-reduce.5.cloned.1.call-start = ((), (), s32[]{:S(2)}) async-start(), calls=%async_computation.4 | async-start | bytes 5242880
Sparse Core Ops, SparseCore 0:
  693.6 741.1 all-reduce.4
where the time goes:
time: 1450 us
  waiting for transfers between devices  899 us (62%)
  blocking collectives  388 us (27%)
  starting transfers between devices  99.9 us (7%)
  other arithmetic  22.6 us (2%)
  local copies, waits for them, and re-layouts  19.5 us (1%)
    unnamed x2, waiting for transfers between devices  737 us
    all_gather x1, blocking collectives, shards(): lax.all_gather(down_rows[0], 'pool', axis=0, tiled=True)  198 us
    all_gather x1, blocking collectives, shards(): lax.all_gather(up_rows[0], 'pool', axis=0, tiled=True)  191 us
    all_to_all x1, waiting for transfers between devices, shards(): lax.all_to_all(ahead_buf, 'pool', split_axis=0, concat_axis=0, tiled=True)  129 us
    all_to_all x1, starting transfers between devices, shards(): lax.all_to_all(back_marks, 'pool', split_axis=0, concat_axis=0, tiled=True)  40 us
  transfers between devices with their start and end apart: 11, of which 5 were waited for; matrix products, arithmetic and copies ran while one was open for 3% of the time, Pallas kernels for 0%

commit v1 on v0

v1 whole, which is shorter than its diff:
```python
import functools

import jax
import jax.numpy as jnp
from jax import lax
from jax.experimental import pallas as pl
from jax.experimental.pallas import tpu as pltpu
from jax.sharding import PartitionSpec as P

SLOTS = 12
TOK = 8
ROWS = SLOTS * TOK
N = 4
D = 5120
R = 64
NC = 5
CW = D // NC
LANE = 640
epsilon = 1e-05
MIB = 1 << 20


class Place:
    def __init__(self):
        section = lax.axis_index("section")
        pool = lax.axis_index("pool")
        self.section, self.pool = section, pool
        self.block, self.core = section // 2, section % 2
        self.x, self.y, self.z = pool // 16, (pool // 4) % 4, pool % 4

    def in_block(self, dx=0, dy=0, dz=0):
        x, y, z = (self.x + dx) % N, (self.y + dy) % N, (self.z + dz) % N
        return {"section": self.section, "pool": x * 16 + y * 4 + z}

    def sibling(self):
        return {"section": self.section + 1 - 2 * self.core, "pool": self.pool}

    def along_z(self, step):
        far = (self.block * N + self.z + step + 4 * N) % (4 * N)
        return {"section": (far // N) * 2 + self.core, "pool": self.pool - self.z + far % N}


def greet(peers):
    barrier = pltpu.get_barrier_semaphore()
    for peer in peers:
        pl.semaphore_signal(barrier, inc=1, device_id=peer, device_id_type=pl.DeviceIdType.MESH)
    pl.semaphore_wait(barrier, len(peers))


def remote(src, dst, send, recv, peer):
    return pltpu.make_async_remote_copy(
        src_ref=src, dst_ref=dst, send_sem=send, recv_sem=recv, device_id=peer, device_id_type=pl.DeviceIdType.MESH
    )


def gather_kernel(own_ref, table_ref, full_ref, tables_ref, local_sems, send_sems, recv_sems):
    me = Place()
    p, x, y, z = me.pool, me.x, me.y, me.z
    greet(
        [me.in_block(dz=1), me.in_block(dz=2), me.in_block(dz=3)]
        + [me.in_block(dy=1), me.in_block(dy=3), me.in_block(dx=1), me.in_block(dx=3)]
    )
    arrays = ((own_ref, full_ref), (table_ref, tables_ref))
    started = []

    def send(a, n, ref, start, count, peer):
        view = ref.at[pl.ds(start, count)]
        copy = remote(view, view, send_sems.at[a, n], recv_sems.at[a, n], peer)
        copy.start()
        started.append(copy)

    def arrive(a, n, ref, start, count, peer):
        view = ref.at[pl.ds(start, count)]
        remote(view, view, send_sems.at[a, n], recv_sems.at[a, n], peer).wait_recv()

    for a, (own, full) in enumerate(arrays):
        for d in (1, 2, 3):
            peer = me.in_block(dz=d)
            copy = remote(own, full.at[p], send_sems.at[a, d], recv_sems.at[a, d], peer)
            copy.start()
            started.append(copy)
        local = pltpu.make_async_copy(own, full.at[p], local_sems.at[a])
        local.start()
        local.wait()
    for a, (own, full) in enumerate(arrays):
        for d in (1, 2, 3):
            arrive(a, d, full, p - z + (z - d + N) % N, 1, me.in_block(dz=d))
    for first, count, coord, up, down in (
        (4, 4, y, me.in_block(dy=1), me.in_block(dy=3)),
        (8, 16, x, me.in_block(dx=1), me.in_block(dx=3)),
    ):
        base = (p // (count * N)) * (count * N)
        here = base + coord * count
        below = base + ((coord + 3) % N) * count
        above = base + ((coord + 1) % N) * count
        across = base + ((coord + 2) % N) * count
        half = count // 2
        for a, (_, full) in enumerate(arrays):
            send(a, first, full, here, count, up)
            send(a, first + 1, full, here, count, down)
        for a, (_, full) in enumerate(arrays):
            arrive(a, first, full, below, count, down)
            send(a, first + 2, full, below, half, up)
            arrive(a, first + 1, full, above, count, up)
            send(a, first + 3, full, above + half, half, down)
        for a, (_, full) in enumerate(arrays):
            arrive(a, first + 2, full, across, half, down)
            arrive(a, first + 3, full, across + half, half, up)
    for copy in started:
        copy.wait_send()


def gather(own, table):
    return pl.pallas_call(
        gather_kernel,
        out_shape=(
            jax.ShapeDtypeStruct((R, 16, LANE), jnp.bfloat16),
            jax.ShapeDtypeStruct((R, 8, 128), jnp.int32),
        ),
        in_specs=[pl.BlockSpec(memory_space=pltpu.VMEM)] * 2,
        out_specs=(pl.BlockSpec(memory_space=pltpu.VMEM),) * 2,
        scratch_shapes=[
            pltpu.SemaphoreType.DMA((2,)),
            pltpu.SemaphoreType.DMA((2, 12)),
            pltpu.SemaphoreType.DMA((2, 12)),
        ],
        compiler_params=pltpu.CompilerParams(
            collective_id=0, has_side_effects=True, vmem_limit_bytes=16 * MIB
        ),
        name="gather",
    )(own, table)


def adapter_kernel(x_ref, g_ref, keep_ref, down_ref, up_ref, gain_ref, routed_ref, gd_ref, gu_ref, normed, through):
    keep = keep_ref[...] > 0.0
    square = jnp.zeros((ROWS, 1), jnp.float32)
    for f in range(NC):
        wide = x_ref[:, f * CW : (f + 1) * CW].astype(jnp.float32)
        square += jnp.sum(wide * wide, axis=1, keepdims=True)
    inv_rms = lax.rsqrt(square * (1.0 / D) + epsilon)
    across = (((1,), (1,)), ((), ()))
    preact = jnp.zeros((ROWS, R), jnp.float32)
    back = jnp.zeros((ROWS, R), jnp.float32)
    for f in range(NC):
        cols = slice(f * CW, (f + 1) * CW)
        wide = x_ref[:, cols].astype(jnp.float32)
        part = (wide * inv_rms * gain_ref[:, cols].astype(jnp.float32)).astype(jnp.bfloat16)
        normed[:, cols] = part
        preact += lax.dot_general(part, down_ref[:, cols], across, preferred_element_type=jnp.float32)
        grad = jnp.where(keep, g_ref[:, cols].astype(jnp.float32), 0.0).astype(jnp.bfloat16)
        back += lax.dot_general(grad, up_ref[:, cols], across, preferred_element_type=jnp.float32)
    gates = jax.nn.sigmoid(preact)
    hidden_wide = (preact * gates).astype(jnp.bfloat16).astype(jnp.float32)
    slope_wide = (back * gates * (1.0 + preact * (1.0 - gates))).astype(jnp.bfloat16).astype(jnp.float32)
    hidden, slope = hidden_wide.astype(jnp.bfloat16), slope_wide.astype(jnp.bfloat16)
    hidden_t, slope_t = hidden_wide.T.astype(jnp.bfloat16), slope_wide.T.astype(jnp.bfloat16)
    centred = jnp.zeros((ROWS, 1), jnp.float32)
    for f in range(NC):
        cols = slice(f * CW, (f + 1) * CW)
        wide = x_ref[:, cols].astype(jnp.float32)
        branch = jnp.dot(hidden, up_ref[:, cols], preferred_element_type=jnp.float32)
        routed_ref[0, f] = jnp.where(keep, wide + branch, 0.0).astype(jnp.bfloat16)
        grad = jnp.where(keep, g_ref[:, cols].astype(jnp.float32), 0.0).astype(jnp.bfloat16)
        gu_ref[:, cols] = jnp.dot(hidden_t, grad, preferred_element_type=jnp.float32).astype(jnp.bfloat16)
        gd_ref[:, cols] = jnp.dot(slope_t, normed[:, cols], preferred_element_type=jnp.float32).astype(jnp.bfloat16)
        part = jnp.dot(slope, down_ref[:, cols], preferred_element_type=jnp.float32)
        part = part * gain_ref[:, cols].astype(jnp.float32)
        through[:, cols] = part
        centred += jnp.sum(part * wide, axis=1, keepdims=True)
    centred = centred * (1.0 / D)
    for f in range(NC):
        cols = slice(f * CW, (f + 1) * CW)
        wide = x_ref[:, cols].astype(jnp.float32)
        grad = jnp.where(keep, g_ref[:, cols].astype(jnp.float32), 0.0)
        inward = grad + inv_rms * (through[:, cols] - wide * inv_rms * inv_rms * centred)
        routed_ref[1, f] = inward.astype(jnp.bfloat16)


def adapter(rows, grads, keep, down_full, up_full, gain_row):
    whole = lambda shape: pl.BlockSpec(shape, lambda i: (0,) * len(shape))
    return pl.pallas_call(
        adapter_kernel,
        grid=(1,),
        out_shape=(
            jax.ShapeDtypeStruct((2, NC, ROWS, CW), jnp.bfloat16),
            jax.ShapeDtypeStruct((R, D), jnp.bfloat16),
            jax.ShapeDtypeStruct((R, D), jnp.bfloat16),
        ),
        in_specs=[
            whole((ROWS, D)),
            whole((ROWS, D)),
            whole((ROWS, 1)),
            whole((R, D)),
            whole((R, D)),
            whole((1, D)),
        ],
        out_specs=(whole((2, NC, ROWS, CW)), whole((R, D)), whole((R, D))),
        scratch_shapes=[pltpu.VMEM((ROWS, D), jnp.bfloat16), pltpu.VMEM((ROWS, D), jnp.float32)],
        compiler_params=pltpu.CompilerParams(vmem_limit_bytes=40 * MIB),
        cost_estimate=pl.CostEstimate(flops=6 * 2 * ROWS * R * D, bytes_accessed=10 * MIB, transcendentals=ROWS * R),
        name="adapter",
    )(rows, grads, keep, down_full, up_full, gain_row)


def repeat_matrix(rows, cols, times, along):
    r = lax.broadcasted_iota(jnp.int32, (rows, cols), 0)
    c = lax.broadcasted_iota(jnp.int32, (rows, cols), 1)
    return ((r // times == c) if along == 0 else (c // times == r)).astype(jnp.bfloat16)


def spread_tokens(small):
    a, b = small.shape
    tall = jnp.dot(repeat_matrix(TOK * a, a, TOK, 0), small, preferred_element_type=jnp.float32).astype(jnp.bfloat16)
    wide = jnp.dot(tall, repeat_matrix(b, TOK * b, TOK, 1), preferred_element_type=jnp.float32)
    r = lax.broadcasted_iota(jnp.int32, (TOK * a, TOK * b), 0) % TOK
    c = lax.broadcasted_iota(jnp.int32, (TOK * a, TOK * b), 1) % TOK
    return jnp.where(r == c, wide, 0.0).astype(jnp.bfloat16)


PAIR = N * N * TOK


def route_kernel(
    src, pick1, pick2, grads,
    ahead_out, behind_out, sums_out,
    lbuf, sbuf, dbuf, h1s, h1r, relay, h2s, mid, last, result, m1, m2,
    rs_mid, rs_send, rs_last, ry_src, ry_mid, ry_last, rz_src, rz_recv, total,
    lrecv, srecv, drecv, lup, ldn, ssend, dsend, swap_send,
    h1send, relay_in, relay_out, h1recv, far_send, mid_recv, near_send, last_recv, out_sem,
    rs_sems, rs_rsems, rz_sems, rz_rsems,
):
    me = Place()
    x, y, z, core = me.x, me.y, me.z, me.core
    o = jnp.where(core == 0, z, 3 - z)
    sibling = me.sibling()
    zup, zdown = me.in_block(dz=1), me.in_block(dz=3)
    znext = me.along_z(1 - 2 * core)
    zprev = me.along_z(2 * core - 1)
    xup, xdown, yup, ydown = me.in_block(dx=1), me.in_block(dx=3), me.in_block(dy=1), me.in_block(dy=3)
    greet([sibling, zup, me.in_block(dz=2), zdown, znext, zprev, xup, xdown, yup, ydown])

    def swap_local(f):
        return remote(src.at[core, f], lbuf.at[f, z], swap_send.at[0, f], lrecv.at[f, z], sibling)

    def swap_cross(f):
        so = 3 - o
        return remote(src.at[1 - core, f], sbuf.at[f, so], swap_send.at[1, f], srecv.at[f, so], sibling)

    def l_up(f, k):
        return remote(lbuf.at[f, k], lbuf.at[f, k], lup.at[f, k], lrecv.at[f, k], zup)

    def l_down(f, k):
        return remote(lbuf.at[f, k], lbuf.at[f, k], ldn.at[f, k], lrecv.at[f, k], zdown)

    def s_next(f, k):
        return remote(sbuf.at[f, k], sbuf.at[f, k], ssend.at[f, k], srecv.at[f, k], znext)

    def s_over(f, k):
        return remote(sbuf.at[f, k], dbuf.at[f, k], ssend.at[f, k], drecv.at[f, k], znext)

    def d_next(f, k):
        return remote(dbuf.at[f, k], dbuf.at[f, k], dsend.at[f, k], drecv.at[f, k], znext)

    half1, half2 = PAIR // 2, ROWS // 2

    def h1_near(r, f, d):
        n = 0 if d == 1 else 1
        return remote(
            h1s.at[r, f, d - 1], h1r.at[r, f, x], h1send.at[r, f, d - 1], h1recv.at[r, f, n], xup if d == 1 else xdown
        )

    def h1_far(r, f, way):
        part = pl.ds(way * half1, half1)
        return remote(
            h1s.at[r, f, 1, part], relay.at[way, r, f], h1send.at[r, f, 3 * way + 1], relay_in.at[way, r, f],
            xdown if way else xup,
        )

    def h1_relay(r, f, way):
        part = pl.ds(way * half1, half1)
        origin = (x + (1 if way else 3)) % N
        return remote(
            relay.at[way, r, f], h1r.at[r, f, origin, part], relay_out.at[way, r, f], h1recv.at[r, f, 2 + way],
            xdown if way else xup,
        )

    def h2_far(r, f, way):
        part = pl.ds(way * half2, half2)
        return remote(
            h2s.at[r, f, 2, part], mid.at[way, r, f], far_send.at[way, r, f], mid_recv.at[way, r, f],
            ydown if way else yup,
        )

    def h2_near(r, f, way):
        return remote(
            h2s.at[r, f, 3 if way else 1], last.at[way, r, f], near_send.at[way, r, f], last_recv.at[way, r, f],
            ydown if way else yup,
        )

    def emit(r, f, out):
        cols = pl.ds(pl.multiple_of(f * CW, 128), CW)
        return pltpu.make_async_copy(result.at[r, f], out.at[:, cols], out_sem.at[r, f])

    def z_begin(f):
        l_up(f, z).wait_recv()

        @pl.when(z < 3)
        def _():
            l_up(f, z).start()

        @pl.when(z > 0)
        def _():
            l_down(f, z).start()

        s_next(f, o).wait_recv()

        @pl.when(o < 3)
        def _():
            s_next(f, o).start()

        @pl.when(o == 3)
        def _():
            s_over(f, o).start()

    def z_rest(f):
        for t in range(1, 8):
            if t <= 3:

                @pl.when(z >= t)
                def _():
                    l_up(f, z - t).wait_recv()

                    @pl.when(z < 3)
                    def _():
                        l_up(f, z - t).start()

                @pl.when(z + t <= 3)
                def _():
                    l_down(f, z + t).wait_recv()

                    @pl.when(z > 0)
                    def _():
                        l_down(f, z + t).start()

                @pl.when(o >= t)
                def _():
                    s_next(f, o - t).wait_recv()

                    @pl.when(o < 3)
                    def _():
                        s_next(f, o - t).start()

                    @pl.when(o == 3)
                    def _():
                        s_over(f, o - t).start()

            @pl.when((o < t) & (t <= o + 4))
            def _():
                k = o + 4 - t
                d_next(f, k).wait_recv()

                @pl.when(o < 3)
                def _():
                    d_next(f, k).start()

    def h1_begin(f):
        for r, buf in ((0, lbuf), (1, dbuf)):
            block = buf[f].reshape(N * ROWS, CW)
            for d in (2, 1, 3, 0):
                to = (x + d) % N
                pick = m1[r, pl.ds(pl.multiple_of(to * PAIR, PAIR), PAIR), :]
                rows = jnp.dot(pick, block, preferred_element_type=jnp.float32).astype(jnp.bfloat16)
                if d == 0:
                    h1r[r, f, x] = rows
                else:
                    h1s[r, f, d - 1] = rows
                if d == 2:
                    h1_far(r, f, 0).start()
                    h1_far(r, f, 1).start()
                elif d:
                    h1_near(r, f, d).start()

    def h1_pass(f):
        for r in (0, 1):
            for way in (0, 1):
                h1_far(r, f, way).wait_recv()
                h1_relay(r, f, way).start()

    def h2_begin(f):
        for r in (0, 1):
            h1_near(r, f, 1).wait_recv()
            h1_near(r, f, 3).wait_recv()
            h1_relay(r, f, 0).wait_recv()
            h1_relay(r, f, 1).wait_recv()
            block = h1r[r, f].reshape(N * PAIR, CW)
            for e in (2, 1, 3, 0):
                to = (y + e) % N
                pick = m2[r, pl.ds(pl.multiple_of(to * ROWS, ROWS), ROWS), :]
                rows = jnp.dot(pick, block, preferred_element_type=jnp.float32).astype(jnp.bfloat16)
                h2s[r, f, e] = rows
                if e == 2:
                    h2_far(r, f, 0).start()
                    h2_far(r, f, 1).start()

    def h2_pass(f):
        for r in (0, 1):
            h2_far(r, f, 0).wait_recv()
            h2s[r, f, 1, :half2] = h2s[r, f, 1, :half2] + mid[0, r, f]
            h2_near(r, f, 0).start()
            h2_far(r, f, 1).wait_recv()
            h2s[r, f, 3, half2:] = h2s[r, f, 3, half2:] + mid[1, r, f]
            h2_near(r, f, 1).start()

    def finish(f):
        for r in (0, 1):
            h2_near(r, f, 0).wait_recv()
            h2_near(r, f, 1).wait_recv()
            result[r, f] = h2s[r, f, 0] + last[0, r, f] + last[1, r, f]

            @pl.when(core == 1 - r)
            def _():
                emit(r, f, ahead_out).start()

            @pl.when(core == r)
            def _():
                emit(r, f, behind_out).start()

    XR, YR = 16 * 16, 4 * 16

    def gsum_far(stage, buf, rows, across, coord, way):
        to = (coord + 2) % N
        dst = (rs_mid, ry_mid)[stage]
        return remote(
            buf.at[pl.ds(to * rows + way * (rows // 2), rows // 2)], dst.at[way],
            rs_sems.at[stage, way], rs_rsems.at[stage, way], across[way],
        )

    def gsum_near(stage, rows, across, way):
        dst = (rs_last, ry_last)[stage]
        return remote(
            rs_send.at[way, pl.ds(0, rows)], dst.at[way],
            rs_sems.at[stage, 2 + way], rs_rsems.at[stage, 2 + way], across[way],
        )

    xs, ys = (xup, xdown), (yup, ydown)

    def gsum_pass(stage, buf, rows, across, coord):
        dst = (rs_mid, ry_mid)[stage]
        h = rows // 2
        for way in (0, 1):
            if stage == 1:
                gsum_near(0, XR, xs, way).wait_send()
            gsum_far(stage, buf, rows, across, coord, way).wait_recv()
            to = (coord + (3 if way else 1)) % N
            base = pl.multiple_of(to * rows, 32)
            first = buf[pl.ds(base, h), :]
            second = buf[pl.ds(pl.multiple_of(base + h, 32), h), :]
            far = dst[way].astype(jnp.float32)
            if way == 0:
                first = (first.astype(jnp.float32) + far).astype(jnp.bfloat16)
            else:
                second = (second.astype(jnp.float32) + far).astype(jnp.bfloat16)
            rs_send[way, pl.ds(0, h), :] = first
            rs_send[way, pl.ds(h, h), :] = second
            gsum_near(stage, rows, across, way).start()

    def gsum_total(stage, buf, rows, across, coord):
        dst = (rs_last, ry_last)[stage]
        for way in (0, 1):
            gsum_near(stage, rows, across, way).wait_recv()
        own = buf[pl.ds(pl.multiple_of(coord * rows, 32), rows), :].astype(jnp.float32)
        return own + dst[0].astype(jnp.float32) + dst[1].astype(jnp.float32)

    def gsum_z(d):
        to = (z + d) % N
        return remote(
            rz_src.at[pl.ds(to * 16, 16)], rz_recv.at[z], rz_sems.at[d], rz_rsems.at[z], me.in_block(dz=d)
        )

    def gsum_z_arrival(d):
        origin = (z + d) % N
        return remote(
            rz_src.at[pl.ds(0, 16)], rz_recv.at[origin], rz_sems.at[d], rz_rsems.at[origin], me.in_block(dz=d)
        )

    def swap(f, _):
        swap_local(f).start()
        swap_cross(f).start()
        return 0

    lax.fori_loop(0, NC, swap, 0)
    gsum_far(0, grads, XR, xs, x, 0).start()
    gsum_far(0, grads, XR, xs, x, 1).start()
    for r in (0, 1):
        m1[r] = spread_tokens(pick1[r])
        m2[r] = spread_tokens(pick2[r])
    z_begin(0)

    def step(n, _):
        @pl.when(n + 1 < NC)
        def _():
            z_begin(n + 1)

        @pl.when(n < NC)
        def _():
            z_rest(n)
            h1_begin(n)

        @pl.when((n >= 1) & (n < NC + 1))
        def _():
            h1_pass(n - 1)

        @pl.when(n == 0)
        def _():
            gsum_pass(0, grads, XR, xs, x)

        @pl.when(n == 1)
        def _():
            ry_src[...] = gsum_total(0, grads, XR, xs, x).astype(jnp.bfloat16)
            gsum_far(1, ry_src, YR, ys, y, 0).start()
            gsum_far(1, ry_src, YR, ys, y, 1).start()

        @pl.when(n == 2)
        def _():
            gsum_pass(1, ry_src, YR, ys, y)

        @pl.when(n == 3)
        def _():
            both = gsum_total(1, ry_src, YR, ys, y)
            rz_src[...] = both.astype(jnp.bfloat16)
            total[...] = both
            for d in (1, 2, 3):
                gsum_z(d).start()

        @pl.when((n >= 2) & (n < NC + 2))
        def _():
            h2_pass(n - 2)

        @pl.when((n >= 1) & (n < NC + 1))
        def _():
            h2_begin(n - 1)

        @pl.when(n >= 3)
        def _():
            finish(n - 3)

        return 0

    lax.fori_loop(0, NC + 3, step, 0)

    acc = total[pl.ds(pl.multiple_of(z * 16, 16), 16), :]
    for d in (1, 2, 3):
        gsum_z_arrival(d).wait_recv()
        acc = acc + rz_recv[(z + d) % N].astype(jnp.float32)
    sums_out[...] = acc

    for way in (0, 1):
        gsum_far(0, grads, XR, xs, x, way).wait_send()
        gsum_far(1, ry_src, YR, ys, y, way).wait_send()
        gsum_near(1, YR, ys, way).wait_send()
    for d in (1, 2, 3):
        gsum_z(d).wait_send()

    def drain(f, _):
        swap_local(f).wait_send()
        swap_cross(f).wait_send()
        for k in range(N):

            @pl.when((z < 3) & (k <= z))
            def _():
                l_up(f, k).wait_send()

            @pl.when((z > 0) & (k >= z))
            def _():
                l_down(f, k).wait_send()

            @pl.when(k <= o)
            def _():
                s_next(f, k).wait_send()

            @pl.when(o < 3)
            def _():
                d_next(f, k).wait_send()

        for r in (0, 1):
            h1_near(r, f, 1).wait_send()
            h1_near(r, f, 3).wait_send()
            for way in (0, 1):
                h1_far(r, f, way).wait_send()
                h1_relay(r, f, way).wait_send()
                h2_far(r, f, way).wait_send()
                h2_near(r, f, way).wait_send()
            emit(r, f, ahead_out).wait()
        return 0

    lax.fori_loop(0, NC, drain, 0)


def route(routed, pick1, pick2, grads):
    bf16, f32 = jnp.bfloat16, jnp.float32
    vmem, dma = pltpu.VMEM, pltpu.SemaphoreType.DMA
    scratch = [
        vmem((NC, N, ROWS, CW), bf16),
        vmem((NC, N, ROWS, CW), bf16),
        vmem((NC, N, ROWS, CW), bf16),
        vmem((2, NC, 3, PAIR, CW), bf16),
        vmem((2, NC, N, PAIR, CW), bf16),
        vmem((2, 2, NC, PAIR // 2, CW), bf16),
        vmem((2, NC, N, ROWS, CW), bf16),
        vmem((2, 2, NC, ROWS // 2, CW), bf16),
        vmem((2, 2, NC, ROWS, CW), bf16),
        vmem((2, NC, ROWS, CW), bf16),
        vmem((2, N * PAIR, N * ROWS), bf16),
        vmem((2, N * ROWS, N * PAIR), bf16),
        vmem((2, 128, LANE), bf16),
        vmem((2, 256, LANE), bf16),
        vmem((2, 256, LANE), bf16),
        vmem((256, LANE), bf16),
        vmem((2, 32, LANE), bf16),
        vmem((2, 64, LANE), bf16),
        vmem((64, LANE), bf16),
        vmem((N, 16, LANE), bf16),
        vmem((64, LANE), f32),
        dma((NC, N)), dma((NC, N)), dma((NC, N)),
        dma((NC, N)), dma((NC, N)), dma((NC, N)), dma((NC, N)),
        dma((2, NC)),
        dma((2, NC, 5)),
        dma((2, 2, NC)), dma((2, 2, NC)),
        dma((2, NC, 4)),
        dma((2, 2, NC)), dma((2, 2, NC)),
        dma((2, 2, NC)), dma((2, 2, NC)),
        dma((2, NC)),
        dma((2, 4)), dma((2, 4)), dma((N,)), dma((N,)),
    ]
    return pl.pallas_call(
        route_kernel,
        out_shape=(
            jax.ShapeDtypeStruct((ROWS, D), bf16),
            jax.ShapeDtypeStruct((ROWS, D), bf16),
            jax.ShapeDtypeStruct((16, LANE), f32),
        ),
        in_specs=[pl.BlockSpec(memory_space=pltpu.VMEM)] * 4,
        out_specs=(
            pl.BlockSpec(memory_space=pl.ANY),
            pl.BlockSpec(memory_space=pl.ANY),
            pl.BlockSpec(memory_space=pltpu.VMEM),
        ),
        scratch_shapes=scratch,
        compiler_params=pltpu.CompilerParams(
            collective_id=1, has_side_effects=True, vmem_limit_bytes=62 * MIB
        ),
        name="route",
    )(routed, pick1, pick2, grads)


def picks(tables, flip):
    me = Place()
    column = lax.dynamic_slice(tables, (me.x * 16 + me.y * 4, 0), (N, SLOTS))
    to = jnp.arange(N * N, dtype=jnp.int32) * 4 + me.z + 1
    source = jnp.arange(N, dtype=jnp.int32)
    place = jnp.where(flip, 3 - source, source)
    hit = column[None, :, None, :] == to[:, None, None, None]
    first = hit & (place[:, None] == source[None, :])[None, :, :, None]
    mine = me.x * 16 + jnp.arange(N, dtype=jnp.int32) * 4 + me.z + 1
    sent = jnp.any(tables[None] == mine[:, None, None], axis=2)
    spot = jnp.cumsum(sent.astype(jnp.int32), axis=1) - 1
    spot = jnp.where(sent, spot, -1).reshape(N, N, N, N)
    spot = lax.dynamic_index_in_dim(spot, me.y, 2, keepdims=False)
    slot = jnp.arange(SLOTS, dtype=jnp.int32)
    second = spot[:, None, :, None, :] == slot[None, :, None, None, None]
    second = second & (source[:, None] == source[None, :])[:, None, None, :, None]
    return (
        first.reshape(N * N * N, N * SLOTS).astype(jnp.bfloat16),
        second.reshape(N * SLOTS, N * N * N).astype(jnp.bfloat16),
    )


def shards(
    activations, cotangents, token_counts, route_ahead, route_back, down_rows, up_rows, norm_gain
):
    sizes = token_counts[0, 0, :SLOTS]
    live = sizes > 0
    entry = jnp.stack(
        [jnp.where(live, route_ahead[0, 0, :SLOTS] + 1, 0), jnp.where(live, route_back[0, 0, :SLOTS] + 1, 0)]
    )
    table = jnp.zeros((8, 128), jnp.int32).at[:2, :SLOTS].set(entry)
    own = jnp.concatenate([down_rows[0, 0].reshape(8, LANE), up_rows[0, 0].reshape(8, LANE)], axis=0)
    full, tables = gather(own, table)
    down_full, up_full = full[:, :8].reshape(R, D), full[:, 8:].reshape(R, D)
    count = lax.axis_size("section")
    from_prev = lax.ppermute(tables[:, 0, :SLOTS], "section", [(s, s + 1) for s in range(count - 1)])
    from_next = lax.ppermute(tables[:, 1, :SLOTS], "section", [(s + 1, s) for s in range(count - 1)])

    rows = activations.reshape(-1, D)
    grads = cotangents.reshape(-1, D)
    keep = (jnp.arange(TOK, dtype=jnp.int32)[None, :] < sizes[:, None]).astype(jnp.float32).reshape(ROWS, 1)
    routed, grad_down, grad_up = adapter(rows, grads, keep, down_full, up_full, norm_gain)

    odd = lax.axis_index("section") % 2 == 1
    local, cross = jnp.where(odd, from_prev, from_next), jnp.where(odd, from_next, from_prev)
    local1, local2 = picks(local, False)
    cross1, cross2 = picks(cross, odd)
    share = jnp.concatenate([grad_down.reshape(R, 8, LANE), grad_up.reshape(R, 8, LANE)], axis=1)
    ahead, behind, sums = route(
        routed, jnp.stack([local1, cross1]), jnp.stack([local2, cross2]), share.reshape(R * 16, LANE)
    )
    shape = (1, 1, SLOTS, TOK, D)
    sums = sums.reshape(2, 1, 1, D)
    return (ahead.reshape(shape), behind.reshape(shape), sums[0], sums[1])


def solution(mesh):
    placed = (
        P("section", "pool", None, None, None),
        P("section", "pool", None, None, None),
        P("section", "pool", None),
        P("section", "pool", None),
        P("section", "pool", None),
        P("section", "pool", None),
        P("section", "pool", None),
        P("section", None),
    )
    return jax.shard_map(
        shards,
        mesh=mesh,
        in_specs=placed,
        out_specs=(
            P("section", "pool", None, None, None),
            P("section", "pool", None, None, None),
            P("section", "pool", None),
            P("section", "pool", None),
        ),
        check_vma=False,
    )
```

time: 1450 us -> 358 us (0.25)
  the two profiles are of different devices: /device:TPU:128 before, /device:TPU:1 now
where the time goes in v1:
time: 358 us; the launch traced here: 353 us
  Pallas kernels  320 us (89%)
  starting transfers between devices  15.9 us (4%)
  local copies, waits for them, and re-layouts  10 us (3%)
  other arithmetic  6.09 us (2%)
    pallas_call x1, Pallas kernels, route(): pl.pallas_call(route_kernel, out_shape=(jax.ShapeDtypeStruct((ROWS, D), b...  288 us
    pallas_call x1, Pallas kernels, gather(): pl.pallas_call(gather_kernel, out_shape=(jax.ShapeDtypeStruct((R, 16, LAN...  29.6 us
    ppermute x1, starting transfers between devices, shards(): lax.ppermute(tables[:, 0, :SLOTS], 'section', [(s, s + 1) for s in range(...  8.71 us
    ppermute x1, starting transfers between devices, shards(): lax.ppermute(tables[:, 1, :SLOTS], 'section', [(s + 1, s) for s in range(...  7.2 us
  transfers between devices with their start and end apart: 2, of which 0 were waited for; matrix products, arithmetic and copies ran while one was open for 1% of the time, Pallas kernels for 1%

profile of v1, /device:TPU:1, one launch (start us, length us, event | category | flops | bytes accessed | tf_op | source)
XLA Modules:
  0.0 352.8 jit_solution(10161888633541752746)
XLA Ops:
  0.6 0.8 reduce.2
  1.5 0.8 reduce.3
  2.3 0.7 fusion.1
  3.0 29.6 %gather.1 = (bf16[64,16,640]{2,1,0:T(8,128)(2,1)S(1)}, s32[64,8,128]{2,1,0:T(8,128)S(1)}) custom-call(bf16[16,640]{1,0:T(8,128)(2,1)S(1)} %pad_maximum_fusion.1.own_ref, s32[8,128]{1,0:T(8,128)S(1)} %scatter.4.table_ref), custom_call_target="tpu_custom_call" | custom-call | tf_op jit(solution)/shard_map/gather/pallas_call | solution.py:114
  32.7 7.2 %collective-permute-start.1 = (s32[64,12]{1,0:T(8,128)S(1)}, s32[64,12]{1,0:T(8,128)S(1)}, u32[]{:S(2)}, u32[]{:S(2)}) collective-permute-start(s32[64,12]{1,0:T(8,128)S(1)} %bitcast.45), channel_id=1, source_target_pairs={{64,0},{128,64},{192,128},{256,192},{320,256},{384,320},{448,384},... | collective-permute-start | bytes 9224 | tf_op jit(solution)/shard_map/ppermute | solution.py:692
  40.0 8.7 %collective-permute-start = (s32[64,12]{1,0:T(8,128)S(1)}, s32[64,12]{1,0:T(8,128)S(1)}, u32[]{:S(2)}, u32[]{:S(2)}) collective-permute-start(s32[64,12]{1,0:T(8,128)S(1)} %slice_bitcast_fusion), channel_id=1, source_target_pairs={{0,64},{64,128},{128,192},{192,256},{256,320},{320,384},{384,448},... | collective-permute-start | bytes 9224 | tf_op jit(solution)/shard_map/ppermute | solution.py:691
  49.0 0.1 fusion.3
  49.3 0.4 copy-done.3
  49.7 0.7 copy-done.1
  50.5 0.4 copy-done.2
  50.8 2.5 adapter.1
  53.4 1.3 copy-done
  54.8 1.2 pad_maximum_fusion
  56.0 0.1 copy.27
  56.4 0.2 reduce_window_sum.17
  56.7 0.2 reduce_window_sum.18
  57.0 0.1 broadcast_and_fusion.3
  57.1 0.1 convert_element_type.65
  57.4 0.1 copy.33
  57.7 0.1 convert_element_type.66
  57.9 0.1 copy.30
  58.1 0.1 broadcast_and_fusion.1
  58.3 0.1 convert_element_type.68
  58.5 0.1 convert_element_type.70
  58.7 0.6 add_convert_fusion.pick1
  59.3 0.6 add_convert_fusion.1.pick2
  59.9 287.6 %route.1 = (bf16[96,5120]{1,0:T(8,128)(2,1)}, bf16[96,5120]{1,0:T(8,128)(2,1)}, f32[16,640]{1,0:T(8,128)}) custom-call(bf16[2,5,96,1024]{3,2,1,0:T(8,128)(2,1)} %copy-done, bf16[2,64,48]{2,1,0:T(8,128)(2,1)} %add_convert_fusion.pick1, bf16[2,48,64]{2,1,0:T(8,128)(2,1)} %add_convert_fusion.1.pick2, bf16[1024,640]{1,0:T(8,128)(2,1)} %bitcast.38), custom_call_target="tpu_custom_call" | custom-call | tf_op jit(solution)/shard_map/route/pallas_call | solution.py:635
  347.5 0.8 fusion.4
  348.4 0.6 squeeze.21
  349.0 0.6 squeeze.20
  349.6 2.2 copy.44
  351.8 0.9 copy.45
  (45 shorter events, 1.8 us)
Async XLA Ops:
  32.7 23.4 %collective-permute-start.1 = (s32[64,12]{1,0:T(8,128)S(1)}, s32[64,12]{1,0:T(8,128)S(1)}, u32[]{:S(2)}, u32[]{:S(2)}) collective-permute-start(s32[64,12]{1,0:T(8,128)S(1)} %bitcast.45), channel_id=1, source_target_pairs={{64,0},{128,64},{192,128},{256,192},{320,256},{384,320},{448,384},... | collective-permute-start | bytes 9224 | tf_op jit(solution)/shard_map/ppermute | solution.py:692
  40.0 16.2 %collective-permute-start = (s32[64,12]{1,0:T(8,128)S(1)}, s32[64,12]{1,0:T(8,128)S(1)}, u32[]{:S(2)}, u32[]{:S(2)}) collective-permute-start(s32[64,12]{1,0:T(8,128)S(1)} %slice_bitcast_fusion), channel_id=1, source_target_pairs={{0,64},{64,128},{128,192},{192,256},{256,320},{320,384},{384,448},... | collective-permute-start | bytes 9224 | tf_op jit(solution)/shard_map/ppermute | solution.py:691
  49.0 0.7 copy-start.3
  49.1 1.3 copy-start.1
  49.1 1.7 copy-start.2
  53.4 1.3 copy-start
  347.5 4.3 %copy-start.4 = (bf16[96,5120]{1,0:T(8,128)(2,1)S(1)}, bf16[96,5120]{1,0:T(8,128)(2,1)}, u32[]{:S(2)}) copy-start(bf16[96,5120]{1,0:T(8,128)(2,1)} %get-tuple-element.30) | copy-start | bytes 2949124

commit v2 on v0

v2 whole, which is shorter than its diff:
```python
import functools

import jax
import jax.numpy as jnp
from jax import lax
from jax.experimental import pallas as pl
from jax.experimental.pallas import tpu as pltpu
from jax.sharding import PartitionSpec as P

SLOTS = 12
TOK = 8
ROWS = SLOTS * TOK
N = 4
D = 5120
R = 64
NC = 5
CW = D // NC
LANE = 640
epsilon = 1e-05
MIB = 1 << 20


class Place:
    def __init__(self):
        section = lax.axis_index("section")
        pool = lax.axis_index("pool")
        self.section, self.pool = section, pool
        self.block, self.core = section // 2, section % 2
        self.x, self.y, self.z = pool // 16, (pool // 4) % 4, pool % 4

    def in_block(self, dx=0, dy=0, dz=0):
        x, y, z = (self.x + dx) % N, (self.y + dy) % N, (self.z + dz) % N
        return {"section": self.section, "pool": x * 16 + y * 4 + z}

    def along_z(self, step):
        far = (self.block * N + self.z + step + 4 * N) % (4 * N)
        return {"section": (far // N) * 2 + self.core, "pool": self.pool - self.z + far % N}


def greet(peers):
    barrier = pltpu.get_barrier_semaphore()
    for peer in peers:
        pl.semaphore_signal(barrier, inc=1, device_id=peer, device_id_type=pl.DeviceIdType.MESH)
    pl.semaphore_wait(barrier, len(peers))


def remote(src, dst, send, recv, peer):
    return pltpu.make_async_remote_copy(
        src_ref=src, dst_ref=dst, send_sem=send, recv_sem=recv, device_id=peer, device_id_type=pl.DeviceIdType.MESH
    )


def gather_kernel(own_ref, table_ref, full_ref, tables_ref, tin, local_sems, tin_send, tin_recv, send_sems, recv_sems):
    me = Place()
    x, y, z = me.x, me.y, me.z
    others = (1, 2, 3)
    to_next = {"section": (me.section + 1) % 8, "pool": me.pool}
    to_prev = {"section": (me.section + 7) % 8, "pool": me.pool}
    along = {
        "x": {d: me.in_block(dx=d) for d in others},
        "y": {d: me.in_block(dy=d) for d in others},
        "z": {d: me.in_block(dz=d) for d in others},
    }
    greet([to_next, to_prev] + [along[axis][d] for axis in "xyz" for d in others])

    crossing = [
        remote(table_ref.at[pl.ds(0, 16)], tin.at[pl.ds(0, 16)], tin_send.at[0], tin_recv.at[0], to_next),
        remote(table_ref.at[pl.ds(16, 16)], tin.at[pl.ds(16, 16)], tin_send.at[1], tin_recv.at[1], to_prev),
    ]
    for copy in crossing:
        copy.start()

    half, k = z // 2, z % 2
    place = jnp.where(half == 0, x * 8 + y * 2, y * 8 + x * 2)
    started = []

    def spread(a, own, full):
        for d in others:
            copy = remote(own, full.at[half, place + k], send_sems.at[a, d], recv_sems.at[a, z], along["z"][d])
            copy.start()
            started.append(copy)
        local = pltpu.make_async_copy(own, full.at[half, place + k], local_sems.at[a])
        local.start()
        local.wait()

    def collect(a, own, full):
        for d in others:
            origin = (z + d) % N
            h, kk = origin // 2, origin % 2
            here = jnp.where(h == 0, x * 8 + y * 2, y * 8 + x * 2) + kk
            remote(own, full.at[h, here], send_sems.at[a, d], recv_sems.at[a, origin], along["z"][d]).wait_recv()

    def stage(a, full, n, wait):
        for h in (0, 1):
            first, second = ((y, x), (x, y))[h]
            axis = ("yx", "xy")[h][n]
            for d in others:
                size = 2 if n == 0 else 8
                at = (second * 8 + first * 2) if n == 0 else second * 8
                sem = 4 + h * 6 + n * 3 + d - 1
                if wait:
                    at = (second * 8 + ((first - d + N) % N) * 2) if n == 0 else ((second - d + N) % N) * 8
                view = full.at[h, pl.ds(at, size)]
                copy = remote(view, view, send_sems.at[a, sem], recv_sems.at[a, sem], along[axis][d])
                if wait:
                    copy.wait_recv()
                else:
                    copy.start()
                    started.append(copy)

    weights = (0, own_ref, full_ref)
    marks = (1, tin, tables_ref)
    spread(*weights)
    for copy in crossing:
        copy.wait_recv()
    spread(*marks)
    collect(*weights)
    stage(0, full_ref, 0, False)
    collect(*marks)
    stage(1, tables_ref, 0, False)
    stage(0, full_ref, 0, True)
    stage(0, full_ref, 1, False)
    stage(1, tables_ref, 0, True)
    stage(1, tables_ref, 1, False)
    stage(0, full_ref, 1, True)
    stage(1, tables_ref, 1, True)
    for copy in crossing + started:
        copy.wait_send()


def gather(own, table):
    dma = pltpu.SemaphoreType.DMA
    return pl.pallas_call(
        gather_kernel,
        out_shape=(
            jax.ShapeDtypeStruct((2, R // 2, 16, LANE), jnp.bfloat16),
            jax.ShapeDtypeStruct((2, R // 2, 32, 128), jnp.bfloat16),
        ),
        in_specs=[pl.BlockSpec(memory_space=pltpu.VMEM)] * 2,
        out_specs=(pl.BlockSpec(memory_space=pltpu.VMEM),) * 2,
        scratch_shapes=[
            pltpu.VMEM((32, 128), jnp.bfloat16), dma((2,)), dma((2,)), dma((2,)), dma((2, 16)), dma((2, 16)),
        ],
        compiler_params=pltpu.CompilerParams(
            collective_id=0, has_side_effects=True, vmem_limit_bytes=16 * MIB
        ),
        name="gather",
    )(own, table)


def adapter_kernel(x_ref, g_ref, keep_ref, down_ref, up_ref, gain_ref, routed_ref, gd_ref, gu_ref, normed, through):
    keep = keep_ref[...] > 0.0
    square = jnp.zeros((ROWS, 1), jnp.float32)
    for f in range(NC):
        wide = x_ref[:, f * CW : (f + 1) * CW].astype(jnp.float32)
        square += jnp.sum(wide * wide, axis=1, keepdims=True)
    inv_rms = lax.rsqrt(square * (1.0 / D) + epsilon)
    across = (((1,), (1,)), ((), ()))
    preact = jnp.zeros((ROWS, R), jnp.float32)
    back = jnp.zeros((ROWS, R), jnp.float32)
    for f in range(NC):
        cols = slice(f * CW, (f + 1) * CW)
        wide = x_ref[:, cols].astype(jnp.float32)
        part = (wide * inv_rms * gain_ref[:, cols].astype(jnp.float32)).astype(jnp.bfloat16)
        normed[:, cols] = part
        preact += lax.dot_general(part, down_ref[:, cols], across, preferred_element_type=jnp.float32)
        grad = jnp.where(keep, g_ref[:, cols].astype(jnp.float32), 0.0).astype(jnp.bfloat16)
        back += lax.dot_general(grad, up_ref[:, cols], across, preferred_element_type=jnp.float32)
    gates = jax.nn.sigmoid(preact)
    hidden_wide = (preact * gates).astype(jnp.bfloat16).astype(jnp.float32)
    slope_wide = (back * gates * (1.0 + preact * (1.0 - gates))).astype(jnp.bfloat16).astype(jnp.float32)
    hidden, slope = hidden_wide.astype(jnp.bfloat16), slope_wide.astype(jnp.bfloat16)
    hidden_t, slope_t = hidden_wide.T.astype(jnp.bfloat16), slope_wide.T.astype(jnp.bfloat16)
    centred = jnp.zeros((ROWS, 1), jnp.float32)
    for f in range(NC):
        cols = slice(f * CW, (f + 1) * CW)
        wide = x_ref[:, cols].astype(jnp.float32)
        branch = jnp.dot(hidden, up_ref[:, cols], preferred_element_type=jnp.float32)
        routed_ref[0, f] = jnp.where(keep, wide + branch, 0.0).astype(jnp.bfloat16)
        grad = jnp.where(keep, g_ref[:, cols].astype(jnp.float32), 0.0).astype(jnp.bfloat16)
        gu_ref[:, cols] = jnp.dot(hidden_t, grad, preferred_element_type=jnp.float32).astype(jnp.bfloat16)
        gd_ref[:, cols] = jnp.dot(slope_t, normed[:, cols], preferred_element_type=jnp.float32).astype(jnp.bfloat16)
        part = jnp.dot(slope, down_ref[:, cols], preferred_element_type=jnp.float32)
        part = part * gain_ref[:, cols].astype(jnp.float32)
        through[:, cols] = part
        centred += jnp.sum(part * wide, axis=1, keepdims=True)
    centred = centred * (1.0 / D)
    for f in range(NC):
        cols = slice(f * CW, (f + 1) * CW)
        wide = x_ref[:, cols].astype(jnp.float32)
        grad = jnp.where(keep, g_ref[:, cols].astype(jnp.float32), 0.0)
        inward = grad + inv_rms * (through[:, cols] - wide * inv_rms * inv_rms * centred)
        routed_ref[1, f] = inward.astype(jnp.bfloat16)


def adapter(rows, grads, keep, down_full, up_full, gain_row):
    whole = lambda shape: pl.BlockSpec(shape, lambda i: (0,) * len(shape))
    return pl.pallas_call(
        adapter_kernel,
        grid=(1,),
        out_shape=(
            jax.ShapeDtypeStruct((2, NC, ROWS, CW), jnp.bfloat16),
            jax.ShapeDtypeStruct((R, D), jnp.bfloat16),
            jax.ShapeDtypeStruct((R, D), jnp.bfloat16),
        ),
        in_specs=[
            whole((ROWS, D)),
            whole((ROWS, D)),
            whole((ROWS, 1)),
            whole((R, D)),
            whole((R, D)),
            whole((1, D)),
        ],
        out_specs=(whole((2, NC, ROWS, CW)), whole((R, D)), whole((R, D))),
        scratch_shapes=[pltpu.VMEM((ROWS, D), jnp.bfloat16), pltpu.VMEM((ROWS, D), jnp.float32)],
        compiler_params=pltpu.CompilerParams(vmem_limit_bytes=40 * MIB),
        cost_estimate=pl.CostEstimate(flops=6 * 2 * ROWS * R * D, bytes_accessed=10 * MIB, transcendentals=ROWS * R),
        name="adapter",
    )(rows, grads, keep, down_full, up_full, gain_row)


def repeat_matrix(rows, cols, times, along):
    r = lax.broadcasted_iota(jnp.int32, (rows, cols), 0)
    c = lax.broadcasted_iota(jnp.int32, (rows, cols), 1)
    return ((r // times == c) if along == 0 else (c // times == r)).astype(jnp.bfloat16)


def spread_tokens(small):
    a, b = small.shape
    tall = jnp.dot(repeat_matrix(TOK * a, a, TOK, 0), small, preferred_element_type=jnp.float32).astype(jnp.bfloat16)
    wide = jnp.dot(tall, repeat_matrix(b, TOK * b, TOK, 1), preferred_element_type=jnp.float32)
    r = lax.broadcasted_iota(jnp.int32, (TOK * a, TOK * b), 0) % TOK
    c = lax.broadcasted_iota(jnp.int32, (TOK * a, TOK * b), 1) % TOK
    return jnp.where(r == c, wide, 0.0).astype(jnp.bfloat16)


PAIR = N * N * TOK
AHEAD = 2


def route_kernel(
    src, pick1, pick2, grads,
    ahead_out, behind_out, sums_out,
    lbuf, dbuf, h1s, h1r, h2s, last, zpart, result, m1, m2,
    g1, g1_sum, g2, g3, total,
    lsend, lrecv, xsend, drecv, dsend, h1send, h1recv, h2send, h2recv, zsend, zrecv, out_sem,
    gsend, grecv,
):
    me = Place()
    x, y, z, core = me.x, me.y, me.z, me.core
    o = jnp.where(core == 0, z, 3 - z)
    znext = me.along_z(1 - 2 * core)
    others = (1, 2, 3)
    along = {"x": {d: me.in_block(dx=d) for d in others}, "y": {d: me.in_block(dy=d) for d in others}}
    zup, zdown = me.in_block(dz=1), me.in_block(dz=3)
    other_core = me.section + 1 - 2 * core

    def facing(d):
        return {"section": other_core, "pool": ((x + d) % N) * 16 + y * 4 + z}

    entry = {
        "section": ((me.block + 2 * core - 1 + N) % N) * 2 + 1 - core,
        "pool": me.pool - z + 3 * (1 - core),
    }
    so = jnp.where(core == 1, z, 3 - z)

    barrier = pltpu.get_barrier_semaphore()

    def hello(peer):
        pl.semaphore_signal(barrier, inc=1, device_id=peer, device_id_type=pl.DeviceIdType.MESH)

    everyone = [me.in_block(dz=d) for d in others] + [along["x"][d] for d in others] + [along["y"][d] for d in others]
    everyone += [znext, me.along_z(2 * core - 1)]
    everyone += [facing(d) for d in range(N)]
    for way in (1, N - 1):
        for k in range(N):
            everyone.append({"section": ((me.block + way) % N) * 2 + 1 - core, "pool": me.pool - z + k})
    for peer in everyone:
        hello(peer)
    pl.semaphore_wait(barrier, len(everyone))

    def local_copy(f, d):
        return remote(src.at[core, f], lbuf.at[f, x], lsend.at[f, d], lrecv.at[f, d], facing(d))

    def cross_copy(f):
        return remote(src.at[1 - core, f], dbuf.at[f, so], xsend.at[f], drecv.at[f, so], entry)

    def cross_pass(f, k):
        return remote(dbuf.at[f, k], dbuf.at[f, k], dsend.at[f, k], drecv.at[f, k], znext)

    def h1_copy(r, f, d):
        return remote(
            h1s.at[r, f, d - 1], h1r.at[r, f, x if r else y], h1send.at[r, f, d - 1], h1recv.at[r, f, d - 1],
            along["x" if r else "y"][d],
        )

    def h2_copy(f, d):
        return remote(h2s.at[1, f, d], last.at[f, d - 1], h2send.at[f, d - 1], h2recv.at[f, d - 1], along["y"][d])

    def z_copy(f, to, way):
        slot = (z - to - 1) if way else (to - z - 1)
        return remote(
            h2s.at[0, f, to], zpart.at[f, way, slot], zsend.at[f, to], zrecv.at[f, way, slot], zdown if way else zup
        )

    def z_arrival(f, slot, way):
        return remote(
            h2s.at[0, f, 0], zpart.at[f, way, slot], zsend.at[f, 0], zrecv.at[f, way, slot], zdown if way else zup
        )

    def emit(r, f, out):
        cols = pl.ds(pl.multiple_of(f * CW, 128), CW)
        return pltpu.make_async_copy(result.at[r, f], out.at[:, cols], out_sem.at[r, f])

    def z_begin(f):
        cross_copy(f).start()
        for d in (2, 1, 3, 0):
            local_copy(f, d).start()

    def z_rest(f):
        for k in (3, 2, 1, 0):
            cross_pass(f, k).wait_recv()

            @pl.when(o < 3)
            def _():
                cross_pass(f, k).start()

    def h1_begin(r, f):
        if r == 0:
            for d in range(N):
                local_copy(f, d).wait_recv()
        here = x if r else y
        block = (dbuf if r else lbuf)[f].reshape(N * ROWS, CW)
        for d in (2, 1, 3, 0):
            to = (here + d) % N
            pick = m1[r, pl.ds(pl.multiple_of(to * PAIR, PAIR), PAIR), :]
            rows = jnp.dot(pick, block, preferred_element_type=jnp.float32).astype(jnp.bfloat16)
            if d == 0:
                h1r[r, f, here] = rows
            else:
                h1s[r, f, d - 1] = rows
                h1_copy(r, f, d).start()

    def h2_begin(r, f):
        for d in others:
            h1_copy(r, f, d).wait_recv()
        block = h1r[r, f].reshape(N * PAIR, CW)
        for d in (2, 1, 3, 0):
            to = (y + d) % N if r else d
            pick = m2[r, pl.ds(pl.multiple_of(to * ROWS, ROWS), ROWS), :]
            h2s[r, f, d] = jnp.dot(pick, block, preferred_element_type=jnp.float32).astype(jnp.bfloat16)
            if r and d:
                h2_copy(f, d).start()
        if r == 0:

            @pl.when(z == 0)
            def _():
                for to in (3, 2, 1):
                    z_copy(f, to, 0).start()

            @pl.when(z == 3)
            def _():
                for to in (0, 1, 2):
                    z_copy(f, to, 1).start()

    def add_on(f, to, way):
        slot = (z - to) if way else (to - z)
        z_arrival(f, slot, way).wait_recv()
        h2s[0, f, to] = h2s[0, f, to] + zpart[f, way, slot]
        z_copy(f, to, way).start()

    def merge_first(f):
        @pl.when(z == 1)
        def _():
            add_on(f, 3, 0)
            add_on(f, 2, 0)

        @pl.when(z == 2)
        def _():
            add_on(f, 0, 1)
            add_on(f, 1, 1)

    def merge_second(f):
        @pl.when(z == 2)
        def _():
            add_on(f, 3, 0)

        @pl.when(z == 1)
        def _():
            add_on(f, 0, 1)

    def hand_out(r, f):
        @pl.when(core == 1 - r)
        def _():
            emit(r, f, ahead_out).start()

        @pl.when(core == r)
        def _():
            emit(r, f, behind_out).start()

    def finish_local(f):
        result[0, f] = h2s[0, f, z]

        @pl.when(z > 0)
        def _():
            z_arrival(f, 0, 0).wait_recv()
            result[0, f] = result[0, f] + zpart[f, 0, 0]

        @pl.when(z < 3)
        def _():
            z_arrival(f, 0, 1).wait_recv()
            result[0, f] = result[0, f] + zpart[f, 1, 0]

        hand_out(0, f)

    def finish_cross(f):
        for d in others:
            h2_copy(f, d).wait_recv()
        result[1, f] = (h2s[1, f, 0] + last[f, 0]) + (last[f, 1] + last[f, 2])
        hand_out(1, f)

    G1, G2, G3 = 128, 32, 16

    def axis_of(n, h):
        return "xy"[(n + h) % 2]

    def at(axis):
        return x if axis == "x" else y

    def g1_copy(h, d):
        axis = axis_of(0, h)
        to = (at(axis) + d) % N
        return remote(
            grads.at[pl.ds(h * 512 + to * G1, G1)], g1.at[h, d - 1], gsend.at[0, h, d - 1], grecv.at[0, h, d - 1],
            along[axis][d],
        )

    def g2_copy(h, d):
        axis = axis_of(1, h)
        to = (at(axis) + d) % N
        return remote(
            g1_sum.at[h, pl.ds(to * G2, G2)], g2.at[h, d - 1], gsend.at[1, h, d - 1], grecv.at[1, h, d - 1],
            along[axis][d],
        )

    def g3_copy(d):
        to = (z + d) % N
        return remote(
            total.at[pl.ds(to * G3, G3)], g3.at[d - 1], gsend.at[2, 0, d - 1], grecv.at[2, 0, d - 1], me.in_block(dz=d)
        )

    def add_three(own, parts):
        return (own + parts[0].astype(jnp.float32)) + (parts[1].astype(jnp.float32) + parts[2].astype(jnp.float32))

    def grads_first():
        for h in (0, 1):
            for d in others:
                g1_copy(h, d).start()

    def grads_second():
        for h in (0, 1):
            for d in others:
                g1_copy(h, d).wait_recv()
            row = pl.multiple_of(h * 512 + at(axis_of(0, h)) * G1, G1)
            g1_sum[h] = add_three(grads[pl.ds(row, G1), :].astype(jnp.float32), g1[h])
            for d in others:
                g2_copy(h, d).start()

    def grads_third():
        for h in (0, 1):
            for d in others:
                g2_copy(h, d).wait_recv()
            row = pl.multiple_of(at(axis_of(1, h)) * G2, G2)
            total[pl.ds(h * G2, G2), :] = add_three(g1_sum[h, pl.ds(row, G2), :], g2[h])
        for d in others:
            g3_copy(d).start()

    def grads_last():
        for d in others:
            g3_copy(d).wait_recv()
        sums_out[...] = add_three(total[pl.ds(pl.multiple_of(z * G3, G3), G3), :], g3[...])

    for f in range(AHEAD):
        z_begin(f)
    grads_first()
    for r in (0, 1):
        m1[r] = spread_tokens(pick1[r])
        m2[r] = spread_tokens(pick2[r])

    def when_chunk(n, lag, run):
        pl.when((n >= lag) & (n < NC + lag))(lambda: run(n - lag))

    def step(n, _):
        when_chunk(n, -AHEAD, z_begin)
        when_chunk(n, 0, lambda f: h1_begin(0, f))
        when_chunk(n, 2, merge_first)
        when_chunk(n, 3, merge_second)
        when_chunk(n, 0, z_rest)
        when_chunk(n, 0, lambda f: h1_begin(1, f))
        when_chunk(n, 1, lambda f: h2_begin(0, f))
        pl.when(n == 1)(grads_second)
        pl.when(n == 2)(grads_third)
        when_chunk(n, 1, lambda f: h2_begin(1, f))
        when_chunk(n, 2, finish_cross)
        when_chunk(n, 4, finish_local)
        return 0

    lax.fori_loop(0, NC + 4, step, 0)
    grads_last()

    for d in others:
        for h in (0, 1):
            g1_copy(h, d).wait_send()
            g2_copy(h, d).wait_send()
        g3_copy(d).wait_send()

    def drain(f, _):
        cross_copy(f).wait_send()
        for d in range(N):
            local_copy(f, d).wait_send()

        for k in range(N):

            @pl.when(o < 3)
            def _():
                cross_pass(f, k).wait_send()

            @pl.when(k < z)
            def _():
                z_copy(f, k, 1).wait_send()

            @pl.when(k > z)
            def _():
                z_copy(f, k, 0).wait_send()

        for d in others:
            h1_copy(0, f, d).wait_send()
            h1_copy(1, f, d).wait_send()
            h2_copy(f, d).wait_send()
        for r in (0, 1):
            emit(r, f, ahead_out).wait()
        return 0

    lax.fori_loop(0, NC, drain, 0)


def route(routed, pick1, pick2, grads):
    bf16, f32 = jnp.bfloat16, jnp.float32
    vmem, dma = pltpu.VMEM, pltpu.SemaphoreType.DMA
    scratch = [
        vmem((NC, N, ROWS, CW), bf16),
        vmem((NC, N, ROWS, CW), bf16),
        vmem((2, NC, 3, PAIR, CW), bf16),
        vmem((2, NC, N, PAIR, CW), bf16),
        vmem((2, NC, N, ROWS, CW), bf16),
        vmem((NC, 3, ROWS, CW), bf16),
        vmem((NC, 2, 3, ROWS, CW), bf16),
        vmem((2, NC, ROWS, CW), bf16),
        vmem((2, N * PAIR, N * ROWS), bf16),
        vmem((2, N * ROWS, N * PAIR), bf16),
        vmem((2, 3, 128, LANE), bf16),
        vmem((2, 128, LANE), f32),
        vmem((2, 3, 32, LANE), f32),
        vmem((3, 16, LANE), f32),
        vmem((64, LANE), f32),
        dma((NC, N)), dma((NC, N)),
        dma((NC,)), dma((NC, N)), dma((NC, N)),
        dma((2, NC, 3)), dma((2, NC, 3)),
        dma((NC, 3)), dma((NC, 3)),
        dma((NC, N)), dma((NC, 2, 3)),
        dma((2, NC)),
        dma((3, 2, 3)), dma((3, 2, 3)),
    ]
    return pl.pallas_call(
        route_kernel,
        out_shape=(
            jax.ShapeDtypeStruct((ROWS, D), bf16),
            jax.ShapeDtypeStruct((ROWS, D), bf16),
            jax.ShapeDtypeStruct((16, LANE), f32),
        ),
        in_specs=[pl.BlockSpec(memory_space=pltpu.VMEM)] * 4,
        out_specs=(
            pl.BlockSpec(memory_space=pl.ANY),
            pl.BlockSpec(memory_space=pl.ANY),
            pl.BlockSpec(memory_space=pltpu.VMEM),
        ),
        scratch_shapes=scratch,
        compiler_params=pltpu.CompilerParams(
            collective_id=1, has_side_effects=True, vmem_limit_bytes=60 * MIB
        ),
        name="route",
    )(routed, pick1, pick2, grads)


def pool_order(halves):
    rest = halves.shape[2:]
    first = halves[0].reshape((N, N, 2) + rest)
    second = jnp.swapaxes(halves[1].reshape((N, N, 2) + rest), 0, 1)
    return jnp.concatenate([first, second], axis=2).reshape((R,) + rest)


def picks(tables, crossing, flip):
    me = Place()
    grid = tables.reshape(N, N, N, SLOTS)
    coord = jnp.arange(N, dtype=jnp.int32)
    same = coord[:, None] == coord[None, :]
    slot = jnp.arange(SLOTS, dtype=jnp.int32)
    if crossing:
        group = grid[me.x, me.y]
        to = jnp.arange(N * N, dtype=jnp.int32) * 4 + me.z + 1
        mine = me.x * 16 + coord * 4 + me.z + 1
        place = jnp.where(flip, 3 - coord, coord)
        hit = (group[None] == to[:, None, None])[:, :, None, :]
        first = hit & (place[:, None] == coord[None, :])[None, :, :, None]
    else:
        group = grid[:, me.y, me.z]
        to = me.x * 16 + jnp.arange(N * N, dtype=jnp.int32).reshape(N, 1, N) + 1
        mine = me.x * 16 + me.y * 4 + coord + 1
        hit = group[None, :, None, :] == to[..., None]
        first = hit[:, :, :, None, :] & same[None, :, None, :, None]
    sent = jnp.any(tables[None] == mine[:, None, None], axis=2)
    spot = jnp.cumsum(sent.astype(jnp.int32), axis=1) - 1
    spot = jnp.where(sent, spot, -1).reshape(N, N, N, N)
    if crossing:
        spot = lax.dynamic_index_in_dim(spot, me.y, 2, keepdims=False)
        second = (spot[:, None, :, None, :] == slot[None, :, None, None, None]) & same[:, None, None, :, None]
    else:
        spot = lax.dynamic_index_in_dim(spot, me.z, 3, keepdims=False)
        spot = jnp.swapaxes(spot, 1, 2)
        second = (spot[:, None, :, :, None] == slot[None, :, None, None, None]) & same[:, None, None, None, :]
    return (
        first.reshape(N * N * N, N * SLOTS).astype(jnp.bfloat16),
        second.reshape(N * SLOTS, N * N * N).astype(jnp.bfloat16),
    )


def shards(
    activations, cotangents, token_counts, route_ahead, route_back, down_rows, up_rows, norm_gain
):
    sizes = token_counts[0, 0, :SLOTS]
    live = sizes > 0
    entry = jnp.stack(
        [jnp.where(live, route_ahead[0, 0, :SLOTS] + 1, 0), jnp.where(live, route_back[0, 0, :SLOTS] + 1, 0)]
    ).astype(jnp.bfloat16)
    table = jnp.pad(entry[:, None, :], ((0, 0), (0, 15), (0, 128 - SLOTS))).reshape(32, 128)
    own = jnp.concatenate([down_rows[0, 0].reshape(8, LANE), up_rows[0, 0].reshape(8, LANE)], axis=0)
    full, tables = gather(own, table)
    full = full.reshape(R, 16, LANE)
    down_full, up_full = full[:, :8].reshape(R, D), full[:, 8:].reshape(R, D)
    section = lax.axis_index("section")
    tables = pool_order(tables[:, :, ::16, :SLOTS].astype(jnp.int32))
    from_prev = jnp.where(section > 0, tables[:, 0], 0)
    from_next = jnp.where(section < lax.axis_size("section") - 1, tables[:, 1], 0)

    rows = activations.reshape(-1, D)
    grads = cotangents.reshape(-1, D)
    keep = (jnp.arange(TOK, dtype=jnp.int32)[None, :] < sizes[:, None]).astype(jnp.float32).reshape(ROWS, 1)
    routed, grad_down, grad_up = adapter(rows, grads, keep, down_full, up_full, norm_gain)

    odd = section % 2 == 1
    local, cross = jnp.where(odd, from_prev, from_next), jnp.where(odd, from_next, from_prev)
    local1, local2 = picks(local, False, False)
    cross1, cross2 = picks(cross, True, odd)
    share = jnp.concatenate([grad_down.reshape(R, 8, LANE), grad_up.reshape(R, 8, LANE)], axis=1)
    ahead, behind, sums = route(
        routed, jnp.stack([local1, cross1]), jnp.stack([local2, cross2]), share.reshape(R * 16, LANE)
    )
    shape = (1, 1, SLOTS, TOK, D)
    sums = sums.reshape(2, 1, 1, D)
    return (ahead.reshape(shape), behind.reshape(shape), sums[0], sums[1])


def solution(mesh):
    placed = (
        P("section", "pool", None, None, None),
        P("section", "pool", None, None, None),
        P("section", "pool", None),
        P("section", "pool", None),
        P("section", "pool", None),
        P("section", "pool", None),
        P("section", "pool", None),
        P("section", None),
    )
    return jax.shard_map(
        shards,
        mesh=mesh,
        in_specs=placed,
        out_specs=(
            P("section", "pool", None, None, None),
            P("section", "pool", None, None, None),
            P("section", "pool", None),
            P("section", "pool", None),
        ),
        check_vma=False,
    )
```

time: 1450 us -> 226 us (0.16)
  the two profiles are of different devices: /device:TPU:128 before, /device:TPU:1 now
where the time goes in v2:
time: 226 us; the launch traced here: 224 us
  Pallas kernels  207 us (92%)
  local copies, waits for them, and re-layouts  10.1 us (4%)
  other arithmetic  6.3 us (3%)
    pallas_call x1, Pallas kernels, route(): pl.pallas_call(route_kernel, out_shape=(jax.ShapeDtypeStruct((ROWS, D), b...  171 us
    pallas_call x1, Pallas kernels, gather(): pl.pallas_call(gather_kernel, out_shape=(jax.ShapeDtypeStruct((2, R // 2,...  32.8 us
    unnamed x16, local copies, waits for them, and re-layouts  5.9 us

profile of v2, /device:TPU:1, one launch (start us, length us, event | category | flops | bytes accessed | tf_op | source)
XLA Modules:
  0.0 224.0 jit_solution(11552439075443372875)
XLA Ops:
  0.7 0.1 copy.30
  0.9 0.7 fusion.9
  1.7 0.8 reduce
  2.5 0.8 reduce.1
  3.5 32.8 %gather.1 = (bf16[2,32,16,640]{3,2,1,0:T(8,128)(2,1)S(1)}, bf16[2,32,32,128]{3,2,1,0:T(8,128)(2,1)S(1)}) custom-call(bf16[16,640]{1,0:T(8,128)(2,1)S(1)} %pad_maximum_fusion.1.own_ref, bf16[32,128]{1,0:T(8,128)(2,1)S(1)} %bitcast.48), custom_call_target="tpu_custom_call" | custom-call | tf_op jit(solution)/shard_map/gather/pallas_call | solution.py:133
  36.2 0.1 fusion.11
  36.6 0.4 slice.43
  37.5 0.2 reduce_window_sum.18
  37.9 0.2 reduce_window_sum.17
  38.2 0.1 broadcast_and_fusion.2
  38.3 0.1 convert_element_type.80
  38.4 0.1 broadcast_and_fusion.3
  38.5 0.1 convert_element_type.79
  38.6 0.6 add_convert_fusion.pick1
  39.4 0.2 copy.41
  39.6 0.1 select_n.180
  39.8 0.1 copy.36
  39.9 0.1 iota_compare_fusion
  40.0 0.1 broadcast_and_fusion.1
  40.1 0.1 convert_element_type.82
  40.3 0.1 convert_element_type.84
  40.6 0.6 add_convert_fusion.1.pick2
  41.2 1.3 copy-done.2
  42.5 2.5 %adapter.1 = (bf16[2,5,96,1024]{3,2,1,0:T(8,128)(2,1)S(1)}, bf16[64,5120]{1,0:T(8,128)(2,1)S(1)}, bf16[64,5120]{1,0:T(8,128)(2,1)S(1)}) custom-call(bf16[128,5120]{1,0:T(8,128)(2,1)S(1)} %bitcast.43, bf16[128,5120]{1,0:T(8,128)(2,1)S(1)} %bitcast.44, f32[96,1]{1,0:T(8,128)S(1)} %reshape.425.keep_ref, bf16[64,5120]{1,0:T(8,128)(2,1)S(1)} %bitcast.42, ...), custom_call_target="tpu_custom_call" | custom-call | flops 377487360 | bytes 10485760 | tf_op jit(solution)/shard_map/adapter/pallas_call | solution.py:198
  45.2 1.1 copy-done
  46.3 1.2 pad_maximum_fusion
  47.5 171.3 %route.1 = (bf16[96,5120]{1,0:T(8,128)(2,1)}, bf16[96,5120]{1,0:T(8,128)(2,1)}, f32[16,640]{1,0:T(8,128)}) custom-call(bf16[2,5,96,1024]{3,2,1,0:T(8,128)(2,1)} %copy-done, bf16[2,64,48]{2,1,0:T(8,128)(2,1)} %add_convert_fusion.pick1, bf16[2,48,64]{2,1,0:T(8,128)(2,1)} %add_convert_fusion.1.pick2, bf16[1024,640]{1,0:T(8,128)(2,1)} %bitcast.49), custom_call_target="tpu_custom_call" | custom-call | tf_op jit(solution)/shard_map/route/pallas_call | solution.py:574
  218.8 0.8 fusion.13
  219.6 0.6 squeeze.19
  220.3 0.6 squeeze.18
  220.9 2.2 copy.50
  223.1 0.9 copy.51
  (48 shorter events, 1.7 us)
Async XLA Ops:
  36.5 4.7 %copy-start.1 = (bf16[1,1,16,8,5120]{4,3,2,1,0:T(8,128)(2,1)S(1)}, bf16[1,1,16,8,5120]{4,3,2,1,0:T(8,128)(2,1)}, u32[]{:S(2)}) copy-start(bf16[1,1,16,8,5120]{4,3,2,1,0:T(8,128)(2,1)} %param.8) | copy-start | bytes 3932164
  36.5 4.7 %copy-start.3 = (bf16[1,5120]{1,0:T(2,128)(2,1)S(1)}, bf16[1,5120]{1,0:T(2,128)(2,1)}, u32[]{:S(2)}) copy-start(bf16[1,5120]{1,0:T(2,128)(2,1)} %gain_ref.1) | copy-start | bytes 30724
  41.2 1.3 copy-start.2
  45.0 1.3 copy-start
  218.8 4.3 %copy-start.4 = (bf16[96,5120]{1,0:T(8,128)(2,1)S(1)}, bf16[96,5120]{1,0:T(8,128)(2,1)}, u32[]{:S(2)}) copy-start(bf16[96,5120]{1,0:T(8,128)(2,1)} %get-tuple-element.18) | copy-start | bytes 2949124

commit v3 on v2

--- a/solution.py
+++ b/solution.py
@@ -13,7 +13,7 @@
 N = 4
 D = 5120
 R = 64
-NC = 5
+NC = 10
 CW = D // NC
 LANE = 640
 epsilon = 1e-05
@@ -50,7 +50,7 @@
     )
 
 
-def gather_kernel(own_ref, table_ref, full_ref, tables_ref, tin, local_sems, tin_send, tin_recv, send_sems, recv_sems):
+def gather_kernel(own_ref, table_ref, full_ref, tables_ref, tin, both, local_sems, tin_send, tin_recv, send_sems, recv_sems):
     me = Place()
     x, y, z = me.x, me.y, me.z
     others = (1, 2, 3)
@@ -109,10 +109,11 @@
                     started.append(copy)
 
     weights = (0, own_ref, full_ref)
-    marks = (1, tin, tables_ref)
+    marks = (1, both, tables_ref)
     spread(*weights)
     for copy in crossing:
         copy.wait_recv()
+    both[...] = tin[:16] + tin[16:]
     spread(*marks)
     collect(*weights)
     stage(0, full_ref, 0, False)
@@ -134,12 +135,13 @@
         gather_kernel,
         out_shape=(
             jax.ShapeDtypeStruct((2, R // 2, 16, LANE), jnp.bfloat16),
-            jax.ShapeDtypeStruct((2, R // 2, 32, 128), jnp.bfloat16),
+            jax.ShapeDtypeStruct((2, R // 2, 16, 128), jnp.bfloat16),
         ),
         in_specs=[pl.BlockSpec(memory_space=pltpu.VMEM)] * 2,
         out_specs=(pl.BlockSpec(memory_space=pltpu.VMEM),) * 2,
         scratch_shapes=[
-            pltpu.VMEM((32, 128), jnp.bfloat16), dma((2,)), dma((2,)), dma((2,)), dma((2, 16)), dma((2, 16)),
+            pltpu.VMEM((32, 128), jnp.bfloat16), pltpu.VMEM((16, 128), jnp.bfloat16),
+            dma((2,)), dma((2,)), dma((2,)), dma((2, 16)), dma((2, 16)),
         ],
         compiler_params=pltpu.CompilerParams(
             collective_id=0, has_side_effects=True, vmem_limit_bytes=16 * MIB
@@ -235,15 +237,29 @@
 
 
 PAIR = N * N * TOK
-AHEAD = 2
+PLAN = (
+    ("cross_start", -2),
+    ("local_start", -3),
+    ("cross_pass", 0),
+    ("merge_first", 4),
+    ("merge_second", 6),
+    ("local_pick", 0),
+    ("cross_pick", 1),
+    ("local_sort", 2),
+    ("grads", 0),
+    ("cross_sort", 3),
+    ("cross_end", 5),
+    ("local_end", 8),
+)
+GRADS = (5, 7, 9)
 
 
 def route_kernel(
-    src, pick1, pick2, grads,
-    ahead_out, behind_out, sums_out,
+    src, local1, local2, cross1, cross2, grads,
+    ahead_out, behind_out, down_out, up_out,
     lbuf, dbuf, h1s, h1r, h2s, last, zpart, result, m1, m2,
     g1, g1_sum, g2, g3, total,
-    lsend, lrecv, xsend, drecv, dsend, h1send, h1recv, h2send, h2recv, zsend, zrecv, out_sem,
+    sent, lrecv, drecv, h1recv, h2recv, zrecv, out_sem,
     gsend, grecv,
 ):
     me = Place()
@@ -280,44 +296,49 @@
     pl.semaphore_wait(barrier, len(everyone))
 
     def local_copy(f, d):
-        return remote(src.at[core, f], lbuf.at[f, x], lsend.at[f, d], lrecv.at[f, d], facing(d))
+        return remote(src.at[core, f], lbuf.at[f, x], sent.at[0], lrecv.at[f], facing(d))
 
     def cross_copy(f):
-        return remote(src.at[1 - core, f], dbuf.at[f, so], xsend.at[f], drecv.at[f, so], entry)
+        return remote(src.at[1 - core, f], dbuf.at[f, so], sent.at[1], drecv.at[f, so], entry)
 
     def cross_pass(f, k):
-        return remote(dbuf.at[f, k], dbuf.at[f, k], dsend.at[f, k], drecv.at[f, k], znext)
+        return remote(dbuf.at[f, k], dbuf.at[f, k], sent.at[2], drecv.at[f, k], znext)
 
     def h1_copy(r, f, d):
         return remote(
-            h1s.at[r, f, d - 1], h1r.at[r, f, x if r else y], h1send.at[r, f, d - 1], h1recv.at[r, f, d - 1],
+            h1s.at[r, f, d - 1], h1r.at[r, f, x if r else y], sent.at[3], h1recv.at[r, f],
             along["x" if r else "y"][d],
         )
 
     def h2_copy(f, d):
-        return remote(h2s.at[1, f, d], last.at[f, d - 1], h2send.at[f, d - 1], h2recv.at[f, d - 1], along["y"][d])
+        return remote(h2s.at[1, f, d], last.at[f, d - 1], sent.at[4], h2recv.at[f], along["y"][d])
 
     def z_copy(f, to, way):
         slot = (z - to - 1) if way else (to - z - 1)
         return remote(
-            h2s.at[0, f, to], zpart.at[f, way, slot], zsend.at[f, to], zrecv.at[f, way, slot], zdown if way else zup
+            h2s.at[0, f, to], zpart.at[f, way, slot], sent.at[5], zrecv.at[f, way, slot], zdown if way else zup
         )
 
     def z_arrival(f, slot, way):
         return remote(
-            h2s.at[0, f, 0], zpart.at[f, way, slot], zsend.at[f, 0], zrecv.at[f, way, slot], zdown if way else zup
+            h2s.at[0, f, 0], zpart.at[f, way, slot], sent.at[5], zrecv.at[f, way, slot], zdown if way else zup
         )
+
+    def arrived(ref, sem):
+        remote(ref, ref, sent.at[0], sem, zup).wait_recv()
+
+    def left(ref, n):
+        remote(ref, ref, sent.at[n], zrecv.at[0, 0, 0], zup).wait_send()
 
     def emit(r, f, out):
         cols = pl.ds(pl.multiple_of(f * CW, 128), CW)
-        return pltpu.make_async_copy(result.at[r, f], out.at[:, cols], out_sem.at[r, f])
-
-    def z_begin(f):
-        cross_copy(f).start()
+        return pltpu.make_async_copy(result.at[r, f], out.at[:, cols], out_sem)
+
+    def local_start(f):
         for d in (2, 1, 3, 0):
             local_copy(f, d).start()
 
-    def z_rest(f):
+    def pass_on(f):
         for k in (3, 2, 1, 0):
             cross_pass(f, k).wait_recv()
 
@@ -327,8 +348,7 @@
 
     def h1_begin(r, f):
         if r == 0:
-            for d in range(N):
-                local_copy(f, d).wait_recv()
+            arrived(lbuf.at[f], lrecv.at[f])
         here = x if r else y
         block = (dbuf if r else lbuf)[f].reshape(N * ROWS, CW)
         for d in (2, 1, 3, 0):
@@ -342,8 +362,7 @@
                 h1_copy(r, f, d).start()
 
     def h2_begin(r, f):
-        for d in others:
-            h1_copy(r, f, d).wait_recv()
+        arrived(h1s.at[r, f], h1recv.at[r, f])
         block = h1r[r, f].reshape(N * PAIR, CW)
         for d in (2, 1, 3, 0):
             to = (y + d) % N if r else d
@@ -414,8 +433,7 @@
         hand_out(0, f)
 
     def finish_cross(f):
-        for d in others:
-            h2_copy(f, d).wait_recv()
+        arrived(last.at[f], h2recv.at[f])
         result[1, f] = (h2s[1, f, 0] + last[f, 0]) + (last[f, 1] + last[f, 2])
         hand_out(1, f)
 
@@ -478,34 +496,41 @@
     def grads_last():
         for d in others:
             g3_copy(d).wait_recv()
-        sums_out[...] = add_three(total[pl.ds(pl.multiple_of(z * G3, G3), G3), :], g3[...])
-
-    for f in range(AHEAD):
-        z_begin(f)
-    grads_first()
-    for r in (0, 1):
-        m1[r] = spread_tokens(pick1[r])
-        m2[r] = spread_tokens(pick2[r])
-
-    def when_chunk(n, lag, run):
-        pl.when((n >= lag) & (n < NC + lag))(lambda: run(n - lag))
-
-    def step(n, _):
-        when_chunk(n, -AHEAD, z_begin)
-        when_chunk(n, 0, lambda f: h1_begin(0, f))
-        when_chunk(n, 2, merge_first)
-        when_chunk(n, 3, merge_second)
-        when_chunk(n, 0, z_rest)
-        when_chunk(n, 0, lambda f: h1_begin(1, f))
-        when_chunk(n, 1, lambda f: h2_begin(0, f))
-        pl.when(n == 1)(grads_second)
-        pl.when(n == 2)(grads_third)
-        when_chunk(n, 1, lambda f: h2_begin(1, f))
-        when_chunk(n, 2, finish_cross)
-        when_chunk(n, 4, finish_local)
+        both = add_three(total[pl.ds(pl.multiple_of(z * G3, G3), G3), :], g3[...])
+        for j in range(8):
+            down_out[:, j * LANE : (j + 1) * LANE] = both[j : j + 1]
+            up_out[:, j * LANE : (j + 1) * LANE] = both[8 + j : 9 + j]
+
+    steps = {
+        "cross_start": lambda f: cross_copy(f).start(),
+        "local_start": local_start,
+        "local_pick": lambda f: h1_begin(0, f),
+        "merge_first": merge_first,
+        "merge_second": merge_second,
+        "cross_pass": pass_on,
+        "cross_pick": lambda f: h1_begin(1, f),
+        "local_sort": lambda f: h2_begin(0, f),
+        "cross_sort": lambda f: h2_begin(1, f),
+        "cross_end": finish_cross,
+        "local_end": finish_local,
+    }
+    for name, lag in PLAN:
+        for f in range(min(-lag, NC)):
+            steps[name](f)
+    for r, (pick1, pick2) in enumerate(((local1, local2), (cross1, cross2))):
+        m1[r] = spread_tokens(pick1[...])
+        m2[r] = spread_tokens(pick2[...])
+
+    def turn(n, _):
+        for name, lag in PLAN:
+            if name == "grads":
+                for when, run in zip(GRADS, (grads_first, grads_second, grads_third)):
+                    pl.when(n == when)(run)
+            elif -lag < NC:
+                pl.when((n >= lag) & (n < NC + lag))(functools.partial(steps[name], n - lag))
         return 0
 
-    lax.fori_loop(0, NC + 4, step, 0)
+    lax.fori_loop(0, NC + max(lag for _, lag in PLAN), turn, 0)
     grads_last()
 
     for d in others:
@@ -514,37 +539,16 @@
             g2_copy(h, d).wait_send()
         g3_copy(d).wait_send()
 
-    def drain(f, _):
-        cross_copy(f).wait_send()
-        for d in range(N):
-            local_copy(f, d).wait_send()
-
-        for k in range(N):
-
-            @pl.when(o < 3)
-            def _():
-                cross_pass(f, k).wait_send()
-
-            @pl.when(k < z)
-            def _():
-                z_copy(f, k, 1).wait_send()
-
-            @pl.when(k > z)
-            def _():
-                z_copy(f, k, 0).wait_send()
-
-        for d in others:
-            h1_copy(0, f, d).wait_send()
-            h1_copy(1, f, d).wait_send()
-            h2_copy(f, d).wait_send()
-        for r in (0, 1):
-            emit(r, f, ahead_out).wait()
-        return 0
-
-    lax.fori_loop(0, NC, drain, 0)
-
-
-def route(routed, pick1, pick2, grads):
+    left(lbuf, 0)
+    left(src.at[0], 1)
+    pl.when(o < 3)(lambda: left(dbuf, 2))
+    left(h1s, 3)
+    left(last, 4)
+    left(last, 5)
+    pltpu.make_async_copy(result, result, out_sem).wait()
+
+
+def route(routed, local1, local2, cross1, cross2, grads):
     bf16, f32 = jnp.bfloat16, jnp.float32
     vmem, dma = pltpu.VMEM, pltpu.SemaphoreType.DMA
     scratch = [
@@ -563,12 +567,10 @@
         vmem((2, 3, 32, LANE), f32),
         vmem((3, 16, LANE), f32),
         vmem((64, LANE), f32),
-        dma((NC, N)), dma((NC, N)),
-        dma((NC,)), dma((NC, N)), dma((NC, N)),
-        dma((2, NC, 3)), dma((2, NC, 3)),
-        dma((NC, 3)), dma((NC, 3)),
-        dma((NC, N)), dma((NC, 2, 3)),
-        dma((2, NC)),
+        dma((6,)),
+        dma((NC,)), dma((NC, N)),
+        dma((2, NC)), dma((NC,)), dma((NC, 2, 3)),
+        dma,
         dma((3, 2, 3)), dma((3, 2, 3)),
     ]
     return pl.pallas_call(
@@ -576,12 +578,14 @@
         out_shape=(
             jax.ShapeDtypeStruct((ROWS, D), bf16),
             jax.ShapeDtypeStruct((ROWS, D), bf16),
-            jax.ShapeDtypeStruct((16, LANE), f32),
+            jax.ShapeDtypeStruct((1, D), f32),
+            jax.ShapeDtypeStruct((1, D), f32),
         ),
-        in_specs=[pl.BlockSpec(memory_space=pltpu.VMEM)] * 4,
+        in_specs=[pl.BlockSpec(memory_space=pltpu.VMEM)] * 6,
         out_specs=(
             pl.BlockSpec(memory_space=pl.ANY),
             pl.BlockSpec(memory_space=pl.ANY),
+            pl.BlockSpec(memory_space=pltpu.VMEM),
             pl.BlockSpec(memory_space=pltpu.VMEM),
         ),
         scratch_shapes=scratch,
@@ -589,7 +593,7 @@
             collective_id=1, has_side_effects=True, vmem_limit_bytes=60 * MIB
         ),
         name="route",
-    )(routed, pick1, pick2, grads)
+    )(routed, local1, local2, cross1, cross2, grads)
 
 
 def pool_order(halves):
@@ -639,16 +643,16 @@
 ):
     sizes = token_counts[0, 0, :SLOTS]
     live = sizes > 0
-    entry = jnp.stack(
-        [jnp.where(live, route_ahead[0, 0, :SLOTS] + 1, 0), jnp.where(live, route_back[0, 0, :SLOTS] + 1, 0)]
-    ).astype(jnp.bfloat16)
-    table = jnp.pad(entry[:, None, :], ((0, 0), (0, 15), (0, 128 - SLOTS))).reshape(32, 128)
+    entry = [jnp.where(live, to[0, 0, :SLOTS] + 1, 0).astype(jnp.bfloat16) for to in (route_ahead, route_back)]
+    table = jnp.concatenate(
+        [jnp.pad(row[None], ((i, 15 - i), (0, 128 - SLOTS))) for i, row in enumerate(entry)], axis=0
+    )
     own = jnp.concatenate([down_rows[0, 0].reshape(8, LANE), up_rows[0, 0].reshape(8, LANE)], axis=0)
     full, tables = gather(own, table)
     full = full.reshape(R, 16, LANE)
     down_full, up_full = full[:, :8].reshape(R, D), full[:, 8:].reshape(R, D)
     section = lax.axis_index("section")
-    tables = pool_order(tables[:, :, ::16, :SLOTS].astype(jnp.int32))
+    tables = pool_order(tables[:, :, :2, :SLOTS].astype(jnp.int32))
     from_prev = jnp.where(section > 0, tables[:, 0], 0)
     from_next = jnp.where(section < lax.axis_size("section") - 1, tables[:, 1], 0)
 
@@ -662,12 +666,9 @@
     local1, local2 = picks(local, False, False)
     cross1, cross2 = picks(cross, True, odd)
     share = jnp.concatenate([grad_down.reshape(R, 8, LANE), grad_up.reshape(R, 8, LANE)], axis=1)
-    ahead, behind, sums = route(
-        routed, jnp.stack([local1, cross1]), jnp.stack([local2, cross2]), share.reshape(R * 16, LANE)
-    )
+    ahead, behind, sum_down, sum_up = route(routed, local1, local2, cross1, cross2, share.reshape(R * 16, LANE))
     shape = (1, 1, SLOTS, TOK, D)
-    sums = sums.reshape(2, 1, 1, D)
-    return (ahead.reshape(shape), behind.reshape(shape), sums[0], sums[1])
+    return (ahead.reshape(shape), behind.reshape(shape), sum_down[None], sum_up[None])
 
 
 def solution(mesh):

time: 226 us -> 206 us (0.912)
  Pallas kernels: 207 us -> 188 us
    pallas_call x1, Pallas kernels: 171 us -> 155 us  [route(): pl.pallas_call(route_kernel, out_shape=(jax.ShapeDtypeStruct((ROWS, D), b...]
    unnamed x16 -> x22, local copies, waits for them, and re-layouts: 5.9 us -> 7.2 us
where the time goes in v3:
time: 206 us
  Pallas kernels  188 us (91%)
  local copies, waits for them, and re-layouts  11.4 us (6%)
  other arithmetic  5.04 us (2%)
    pallas_call x1, Pallas kernels, route(): pl.pallas_call(route_kernel, out_shape=(jax.ShapeDtypeStruct((ROWS, D), b...  155 us
    pallas_call x1, Pallas kernels, gather(): pl.pallas_call(gather_kernel, out_shape=(jax.ShapeDtypeStruct((2, R // 2,...  31 us
    unnamed x22, local copies, waits for them, and re-layouts  7.2 us

profile of v3, /device:TPU:1, one launch (start us, length us, event | category | flops | bytes accessed | tf_op | source)
XLA Modules:
  0.0 205.7 jit_solution(12698948954935188851)
XLA Ops:
  0.7 0.1 copy.30
  0.9 0.7 fusion.7
  1.7 0.8 reduce
  2.5 0.8 reduce.1
  3.5 31.0 %gather.1 = (bf16[2,32,16,640]{3,2,1,0:T(8,128)(2,1)S(1)}, bf16[2,32,16,128]{3,2,1,0:T(8,128)(2,1)S(1)}) custom-call(bf16[16,640]{1,0:T(8,128)(2,1)S(1)} %pad_maximum_fusion.1.own_ref, bf16[32,128]{1,0:T(8,128)(2,1)S(1)} %fusion.4.table_ref), custom_call_target="tpu_custom_call" | custom-call | tf_op jit(solution)/shard_map/gather/pallas_call | solution.py:134
  34.5 0.1 fusion.10
  35.4 0.2 reduce_window_sum.17
  35.7 0.1 compare_reduce_fusion
  35.8 0.2 reduce_window_sum.18
  36.1 0.1 select_n.188
  36.2 0.1 copy.36
  36.3 0.1 select_n.180
  36.5 0.2 copy.41
  36.7 0.1 iota_compare_fusion
  36.8 0.1 and_convert_fusion.1
  36.9 0.7 reshape.357.cross1
  37.6 0.1 and_convert_fusion.3
  37.7 0.7 reshape.355.local1
  38.5 0.1 and_convert_fusion
  38.6 0.1 reshape.358
  38.7 0.7 copy.38.cross2
  39.4 0.1 reshape.356
  39.5 0.7 copy.37.local2
  40.2 1.3 copy-done.2
  41.5 2.5 %adapter.1 = (bf16[2,10,96,512]{3,2,1,0:T(8,128)(2,1)S(1)}, bf16[64,5120]{1,0:T(8,128)(2,1)S(1)}, bf16[64,5120]{1,0:T(8,128)(2,1)S(1)}) custom-call(bf16[128,5120]{1,0:T(8,128)(2,1)S(1)} %bitcast.48, bf16[128,5120]{1,0:T(8,128)(2,1)S(1)} %bitcast.49, f32[96,1]{1,0:T(8,128)S(1)} %reshape.359.keep_ref, bf16[64,5120]{1,0:T(8,128)(2,1)S(1)} %bitcast.47, ...), custom_call_target="tpu_custom_call" | custom-call | flops 377487360 | bytes 10485760 | tf_op jit(solution)/shard_map/adapter/pallas_call | solution.py:200
  44.2 1.1 copy-done
  45.3 1.2 pad_maximum_fusion
  46.5 154.8 %route.1 = (bf16[96,5120]{1,0:T(8,128)(2,1)}, bf16[96,5120]{1,0:T(8,128)(2,1)}, f32[1,5120]{1,0:T(1,128)}, f32[1,5120]{1,0:T(1,128)}) custom-call(bf16[2,10,96,512]{3,2,1,0:T(8,128)(2,1)} %copy-done, bf16[64,48]{1,0:T(8,128)(2,1)} %reshape.355.local1, bf16[48,64]{1,0:T(8,128)(2,1)} %copy.37.local2, bf16[64,48]{1,0:T(8,128)(2,1)} %reshape.357.cross1, ...), custom_call_target="tpu_custom_call" | custom-call | tf_op jit(solution)/shard_map/route/pallas_call | solution.py:576
  201.3 2.3 %copy.52 = bf16[1,1,12,8,5120]{4,3,2,1,0:T(8,128)(2,1)} copy(bf16[1,1,12,8,5120]{4,3,2,1,0:T(8,128)(2,1)} %bitcast.59) | data formatting | bytes 1966080
  203.6 0.9 copy.53
  204.5 0.6 copy.54
  205.1 0.6 copy.55
  (48 shorter events, 1.3 us)
Async XLA Ops:
  34.7 5.5 %copy-start.1 = (bf16[1,1,16,8,5120]{4,3,2,1,0:T(8,128)(2,1)S(1)}, bf16[1,1,16,8,5120]{4,3,2,1,0:T(8,128)(2,1)}, u32[]{:S(2)}) copy-start(bf16[1,1,16,8,5120]{4,3,2,1,0:T(8,128)(2,1)} %param.8) | copy-start | bytes 3932164
  34.7 5.5 %copy-start.3 = (bf16[1,5120]{1,0:T(2,128)(2,1)S(1)}, bf16[1,5120]{1,0:T(2,128)(2,1)}, u32[]{:S(2)}) copy-start(bf16[1,5120]{1,0:T(2,128)(2,1)} %gain_ref.1) | copy-start | bytes 30724
  40.2 1.3 copy-start.2
  44.0 1.3 copy-start
  201.3 2.3 %copy-start.4 = (bf16[96,5120]{1,0:T(8,128)(2,1)S(1)}, bf16[96,5120]{1,0:T(8,128)(2,1)}, u32[]{:S(2)}) copy-start(bf16[96,5120]{1,0:T(8,128)(2,1)} %get-tuple-element.19) | copy-start | bytes 2949124
  203.6 1.0 copy-start.6
  203.6 1.6 copy-start.5

commit v4 on v3

--- a/solution.py
+++ b/solution.py
@@ -50,7 +50,7 @@
     )
 
 
-def gather_kernel(own_ref, table_ref, full_ref, tables_ref, tin, both, local_sems, tin_send, tin_recv, send_sems, recv_sems):
+def gather_kernel(own_ref, table_ref, full_ref, tables_ref, tin, both, tin_send, tin_recv, send_sems, recv_sems):
     me = Place()
     x, y, z = me.x, me.y, me.z
     others = (1, 2, 3)
@@ -72,41 +72,34 @@
 
     half, k = z // 2, z % 2
     place = jnp.where(half == 0, x * 8 + y * 2, y * 8 + x * 2)
-    started = []
 
     def spread(a, own, full):
         for d in others:
-            copy = remote(own, full.at[half, place + k], send_sems.at[a, d], recv_sems.at[a, z], along["z"][d])
-            copy.start()
-            started.append(copy)
-        local = pltpu.make_async_copy(own, full.at[half, place + k], local_sems.at[a])
-        local.start()
-        local.wait()
+            remote(own, full.at[half, place + k], send_sems.at[a, 0], recv_sems.at[a, 0], along["z"][d]).start()
+        full[half, place + k] = own[...]
+
+    def group(a, full, n, size, h, wait):
+        view = full.at[h, pl.ds(0, 3 * size)]
+        sem = 0 if n < 0 else 1 + 2 * n + h
+        copy = remote(view, view, send_sems.at[a, sem], recv_sems.at[a, sem], along["z"][1])
+        copy.wait_recv() if wait else copy.wait_send()
 
     def collect(a, own, full):
-        for d in others:
-            origin = (z + d) % N
-            h, kk = origin // 2, origin % 2
-            here = jnp.where(h == 0, x * 8 + y * 2, y * 8 + x * 2) + kk
-            remote(own, full.at[h, here], send_sems.at[a, d], recv_sems.at[a, origin], along["z"][d]).wait_recv()
+        group(a, full, -1, 1, 0, True)
 
     def stage(a, full, n, wait):
+        size = (2, 8)[n]
         for h in (0, 1):
             first, second = ((y, x), (x, y))[h]
             axis = ("yx", "xy")[h][n]
-            for d in others:
-                size = 2 if n == 0 else 8
-                at = (second * 8 + first * 2) if n == 0 else second * 8
-                sem = 4 + h * 6 + n * 3 + d - 1
-                if wait:
-                    at = (second * 8 + ((first - d + N) % N) * 2) if n == 0 else ((second - d + N) % N) * 8
+            at = (second * 8 + first * 2) if n == 0 else second * 8
+            if wait:
+                group(a, full, n, size, h, True)
+                continue
+            for d in (2, 1, 3):
                 view = full.at[h, pl.ds(at, size)]
-                copy = remote(view, view, send_sems.at[a, sem], recv_sems.at[a, sem], along[axis][d])
-                if wait:
-                    copy.wait_recv()
-                else:
-                    copy.start()
-                    started.append(copy)
+                sem = 1 + 2 * n + h
+                remote(view, view, send_sems.at[a, sem], recv_sems.at[a, sem], along[axis][d]).start()
 
     weights = (0, own_ref, full_ref)
     marks = (1, both, tables_ref)
@@ -125,8 +118,13 @@
     stage(1, tables_ref, 1, False)
     stage(0, full_ref, 1, True)
     stage(1, tables_ref, 1, True)
-    for copy in crossing + started:
+    for copy in crossing:
         copy.wait_send()
+    for a, full in ((0, full_ref), (1, tables_ref)):
+        group(a, full, -1, 1, 0, False)
+        for n, size in ((0, 2), (1, 8)):
+            for h in (0, 1):
+                group(a, full, n, size, h, False)
 
 
 def gather(own, table):
@@ -141,7 +139,7 @@
         out_specs=(pl.BlockSpec(memory_space=pltpu.VMEM),) * 2,
         scratch_shapes=[
             pltpu.VMEM((32, 128), jnp.bfloat16), pltpu.VMEM((16, 128), jnp.bfloat16),
-            dma((2,)), dma((2,)), dma((2,)), dma((2, 16)), dma((2, 16)),
+            dma((2,)), dma((2,)), dma((2, 5)), dma((2, 5)),
         ],
         compiler_params=pltpu.CompilerParams(
             collective_id=0, has_side_effects=True, vmem_limit_bytes=16 * MIB
@@ -251,7 +249,7 @@
     ("cross_end", 5),
     ("local_end", 8),
 )
-GRADS = (5, 7, 9)
+GRADS = (3, 5, 7)
 
 
 def route_kernel(
@@ -517,9 +515,23 @@
     for name, lag in PLAN:
         for f in range(min(-lag, NC)):
             steps[name](f)
-    for r, (pick1, pick2) in enumerate(((local1, local2), (cross1, cross2))):
-        m1[r] = spread_tokens(pick1[...])
-        m2[r] = spread_tokens(pick2[...])
+    for r, (receivers, spots) in enumerate(((local1, local2), (cross1, cross2))):
+        i = lax.broadcasted_iota(jnp.int32, (N * N * N, N * SLOTS), 0)
+        c = lax.broadcasted_iota(jnp.int32, (N * N * N, N * SLOTS), 1) // SLOTS
+        if r:
+            to, fits = (i // N) * N + z, i % N == jnp.where(core == 1, 3 - c, c)
+        else:
+            to, fits = x * 16 + (i // 16) * N + i % N, (i // N) % N == c
+        hit = fits & (receivers[...] == (to + 1).astype(jnp.float32))
+        m1[r] = spread_tokens(jnp.where(hit, 1.0, 0.0).astype(jnp.bfloat16))
+        i = lax.broadcasted_iota(jnp.int32, (N * SLOTS, N * N * N), 0)
+        c = lax.broadcasted_iota(jnp.int32, (N * SLOTS, N * N * N), 1)
+        spot = jnp.dot(
+            repeat_matrix(N * SLOTS, N, SLOTS, 0), spots[...].astype(jnp.bfloat16), preferred_element_type=jnp.float32
+        )
+        fits = i // SLOTS == ((c // N) % N if r else c % N)
+        hit = fits & (spot == (i % SLOTS).astype(jnp.float32))
+        m2[r] = spread_tokens(jnp.where(hit, 1.0, 0.0).astype(jnp.bfloat16))
 
     def turn(n, _):
         for name, lag in PLAN:
@@ -590,7 +602,7 @@
         ),
         scratch_shapes=scratch,
         compiler_params=pltpu.CompilerParams(
-            collective_id=1, has_side_effects=True, vmem_limit_bytes=60 * MIB
+            collective_id=1, has_side_effects=True, vmem_limit_bytes=48 * MIB
         ),
         name="route",
     )(routed, local1, local2, cross1, cross2, grads)
@@ -603,39 +615,25 @@
     return jnp.concatenate([first, second], axis=2).reshape((R,) + rest)
 
 
-def picks(tables, crossing, flip):
+def picks(tables, crossing):
     me = Place()
     grid = tables.reshape(N, N, N, SLOTS)
     coord = jnp.arange(N, dtype=jnp.int32)
-    same = coord[:, None] == coord[None, :]
-    slot = jnp.arange(SLOTS, dtype=jnp.int32)
     if crossing:
-        group = grid[me.x, me.y]
-        to = jnp.arange(N * N, dtype=jnp.int32) * 4 + me.z + 1
-        mine = me.x * 16 + coord * 4 + me.z + 1
-        place = jnp.where(flip, 3 - coord, coord)
-        hit = (group[None] == to[:, None, None])[:, :, None, :]
-        first = hit & (place[:, None] == coord[None, :])[None, :, :, None]
+        group, mine = grid[me.x, me.y], me.x * 16 + coord * 4 + me.z + 1
+        group = jnp.where(me.core == 1, group[::-1], group)
     else:
-        group = grid[:, me.y, me.z]
-        to = me.x * 16 + jnp.arange(N * N, dtype=jnp.int32).reshape(N, 1, N) + 1
-        mine = me.x * 16 + me.y * 4 + coord + 1
-        hit = group[None, :, None, :] == to[..., None]
-        first = hit[:, :, :, None, :] & same[None, :, None, :, None]
+        group, mine = grid[:, me.y, me.z], me.x * 16 + me.y * 4 + coord + 1
     sent = jnp.any(tables[None] == mine[:, None, None], axis=2)
     spot = jnp.cumsum(sent.astype(jnp.int32), axis=1) - 1
-    spot = jnp.where(sent, spot, -1).reshape(N, N, N, N)
+    spot = jnp.where(sent, spot, -1).astype(jnp.float32).reshape(N, N, N, N)
     if crossing:
-        spot = lax.dynamic_index_in_dim(spot, me.y, 2, keepdims=False)
-        second = (spot[:, None, :, None, :] == slot[None, :, None, None, None]) & same[:, None, None, :, None]
+        spot = lax.dynamic_index_in_dim(spot, me.y, 2, keepdims=True)
     else:
-        spot = lax.dynamic_index_in_dim(spot, me.z, 3, keepdims=False)
+        spot = lax.dynamic_index_in_dim(spot, me.z, 3, keepdims=True)
         spot = jnp.swapaxes(spot, 1, 2)
-        second = (spot[:, None, :, :, None] == slot[None, :, None, None, None]) & same[:, None, None, None, :]
-    return (
-        first.reshape(N * N * N, N * SLOTS).astype(jnp.bfloat16),
-        second.reshape(N * SLOTS, N * N * N).astype(jnp.bfloat16),
-    )
+    spot = jnp.broadcast_to(spot, (N, N, N, N)).reshape(N, N * N * N)
+    return group.astype(jnp.float32).reshape(1, N * SLOTS), spot
 
 
 def shards(
@@ -647,7 +645,7 @@
     table = jnp.concatenate(
         [jnp.pad(row[None], ((i, 15 - i), (0, 128 - SLOTS))) for i, row in enumerate(entry)], axis=0
     )
-    own = jnp.concatenate([down_rows[0, 0].reshape(8, LANE), up_rows[0, 0].reshape(8, LANE)], axis=0)
+    own = jnp.stack([down_rows[0, 0], up_rows[0, 0]]).reshape(16, LANE)
     full, tables = gather(own, table)
     full = full.reshape(R, 16, LANE)
     down_full, up_full = full[:, :8].reshape(R, D), full[:, 8:].reshape(R, D)
@@ -663,8 +661,8 @@
 
     odd = section % 2 == 1
     local, cross = jnp.where(odd, from_prev, from_next), jnp.where(odd, from_next, from_prev)
-    local1, local2 = picks(local, False, False)
-    cross1, cross2 = picks(cross, True, odd)
+    local1, local2 = picks(local, False)
+    cross1, cross2 = picks(cross, True)
     share = jnp.concatenate([grad_down.reshape(R, 8, LANE), grad_up.reshape(R, 8, LANE)], axis=1)
     ahead, behind, sum_down, sum_up = route(routed, local1, local2, cross1, cross2, share.reshape(R * 16, LANE))
     shape = (1, 1, SLOTS, TOK, D)

time: 206 us -> 193 us (0.937)
  local copies, waits for them, and re-layouts: 11.4 us -> 6.14 us
  Pallas kernels: 188 us -> 183 us
  other arithmetic: 5.04 us -> 2.53 us
    pallas_call x1, Pallas kernels: 155 us -> 149 us  [route(): pl.pallas_call(route_kernel, out_shape=(jax.ShapeDtypeStruct((ROWS, D), b...]
    convert_element_type x6 -> x3, local copies, waits for them, and re-layouts: 3.01 us -> 0.29 us  [the longest x2 0.2 us: picks(): spot = jnp.where(sent, spot, -1).astype(jnp.float32).reshape(N, N, N, N)]
    unnamed x22 -> x15, local copies, waits for them, and re-layouts: 7.2 us -> 4.94 us
where the time goes in v4:
time: 193 us
  Pallas kernels  183 us (95%)
  local copies, waits for them, and re-layouts  6.14 us (3%)
  other arithmetic  2.53 us (1%)
    pallas_call x1, Pallas kernels, route(): pl.pallas_call(route_kernel, out_shape=(jax.ShapeDtypeStruct((ROWS, D), b...  149 us
    pallas_call x1, Pallas kernels, gather(): pl.pallas_call(gather_kernel, out_shape=(jax.ShapeDtypeStruct((2, R // 2,...  31.8 us
    unnamed x15, local copies, waits for them, and re-layouts  4.94 us

profile of v4, /device:TPU:1, one launch (start us, length us, event | category | flops | bytes accessed | tf_op | source)
XLA Modules:
  0.0 193.0 jit_solution(9500995591266582279)
XLA Ops:
  0.7 0.7 fusion.7
  1.5 0.8 pad_maximum_fusion.1
  2.3 0.1 reshape.240.keep_ref
  2.4 31.8 %gather.1 = (bf16[2,32,16,640]{3,2,1,0:T(8,128)(2,1)S(1)}, bf16[2,32,16,128]{3,2,1,0:T(8,128)(2,1)S(1)}) custom-call(bf16[16,640]{1,0:T(8,128)(2,1)S(1)} %reshape.226.own_ref, bf16[32,128]{1,0:T(8,128)(2,1)S(1)} %fusion.4.table_ref), custom_call_target="tpu_custom_call" | custom-call | tf_op jit(solution)/shard_map/gather/pallas_call | solution.py:132
  34.3 0.1 fusion.10
  34.4 0.1 copy.31
  34.5 0.1 copy.30
  34.8 0.1 convert_element_type.90.local1
  34.9 0.1 reshape.232.cross1
  35.0 0.1 copy.24
  35.1 0.1 compare_reduce_fusion.1
  35.2 0.2 reduce_window_sum.17
  35.4 0.1 copy.26
  35.5 0.1 compare_reduce_fusion
  35.6 0.2 reduce_window_sum.18
  35.9 0.1 convert_element_type.97
  36.0 0.1 reshape.233.cross2
  36.1 0.1 convert_element_type.93
  36.2 0.1 constant_dynamic-slice_fusion.1
  36.3 0.2 copy.28
  36.5 0.1 broadcast_in_dim.40
  36.6 0.1 reshape.231.local2
  36.7 1.3 copy-done.1
  38.0 2.5 %adapter.1 = (bf16[2,10,96,512]{3,2,1,0:T(8,128)(2,1)S(1)}, bf16[64,5120]{1,0:T(8,128)(2,1)S(1)}, bf16[64,5120]{1,0:T(8,128)(2,1)S(1)}) custom-call(bf16[128,5120]{1,0:T(8,128)(2,1)S(1)} %bitcast.47, bf16[128,5120]{1,0:T(8,128)(2,1)S(1)} %bitcast.48, f32[96,1]{1,0:T(8,128)S(1)} %reshape.240.keep_ref, bf16[64,5120]{1,0:T(8,128)(2,1)S(1)} %bitcast.46, ...), custom_call_target="tpu_custom_call" | custom-call | flops 377487360 | bytes 10485760 | tf_op jit(solution)/shard_map/adapter/pallas_call | solution.py:198
  40.5 0.1 copy.32
  40.6 0.1 copy.33
  40.7 0.1 pad_maximum_fusion
  40.8 149.0 %route.1 = (bf16[96,5120]{1,0:T(8,128)(2,1)S(1)}, bf16[96,5120]{1,0:T(8,128)(2,1)S(1)}, f32[1,5120]{1,0:T(1,128)S(1)}, f32[1,5120]{1,0:T(1,128)S(1)}) custom-call(bf16[2,10,96,512]{3,2,1,0:T(8,128)(2,1)S(1)} %get-tuple-element.14.src, f32[1,48]{1,0:T(1,128)S(1)} %convert_element_type.90.local1, f32[4,64]{1,0:T(4,128)S(1)} %reshape.231.local2, ...), custom_call_target="tpu_custom_call" | custom-call | tf_op jit(solution)/shard_map/route/pallas_call | solution.py:588
  189.9 0.9 copy.40
  190.8 0.9 copy.41
  191.7 0.6 copy.42
  192.4 0.6 copy.43
  (26 shorter events, 0.4 us)
Async XLA Ops:
  34.5 2.2 %copy-start = (bf16[1,1,16,8,5120]{4,3,2,1,0:T(8,128)(2,1)S(1)}, bf16[1,1,16,8,5120]{4,3,2,1,0:T(8,128)(2,1)}, u32[]{:S(2)}) copy-start(bf16[1,1,16,8,5120]{4,3,2,1,0:T(8,128)(2,1)} %param.8) | copy-start | bytes 3932164
  34.5 2.2 %copy-start.2 = (bf16[1,5120]{1,0:T(2,128)(2,1)S(1)}, bf16[1,5120]{1,0:T(2,128)(2,1)}, u32[]{:S(2)}) copy-start(bf16[1,5120]{1,0:T(2,128)(2,1)} %gain_ref.1) | copy-start | bytes 30724
  36.7 1.3 copy-start.1

commit v5 on v4

--- a/solution.py
+++ b/solution.py
@@ -249,7 +249,7 @@
     ("cross_end", 5),
     ("local_end", 8),
 )
-GRADS = (3, 5, 7)
+GRADS = (2, 4, 6)
 
 
 def route_kernel(

time: 193 us -> 193 us (level)
  no operation moved by 1% of the time
where the time goes in v5:
time: 193 us; the launch traced here: 192 us
  Pallas kernels  182 us (94%)
  local copies, waits for them, and re-layouts  6.14 us (3%)
  other arithmetic  2.53 us (1%)
    pallas_call x1, Pallas kernels, route(): pl.pallas_call(route_kernel, out_shape=(jax.ShapeDtypeStruct((ROWS, D), b...  148 us
    pallas_call x1, Pallas kernels, gather(): pl.pallas_call(gather_kernel, out_shape=(jax.ShapeDtypeStruct((2, R // 2,...  31.8 us
    unnamed x15, local copies, waits for them, and re-layouts  4.94 us

profile of v5, /device:TPU:1, one launch (start us, length us, event | category | flops | bytes accessed | tf_op | source)
XLA Modules:
  0.0 191.8 jit_solution(8675481007734144619)
XLA Ops:
  0.7 0.7 fusion.7
  1.5 0.8 pad_maximum_fusion.1
  2.3 0.1 reshape.240.keep_ref
  2.4 31.8 %gather.1 = (bf16[2,32,16,640]{3,2,1,0:T(8,128)(2,1)S(1)}, bf16[2,32,16,128]{3,2,1,0:T(8,128)(2,1)S(1)}) custom-call(bf16[16,640]{1,0:T(8,128)(2,1)S(1)} %reshape.226.own_ref, bf16[32,128]{1,0:T(8,128)(2,1)S(1)} %fusion.4.table_ref), custom_call_target="tpu_custom_call" | custom-call | tf_op jit(solution)/shard_map/gather/pallas_call | solution.py:132
  34.3 0.1 fusion.10
  34.4 0.1 copy.31
  34.5 0.1 copy.30
  34.8 0.1 convert_element_type.90.local1
  34.9 0.1 reshape.232.cross1
  35.0 0.1 copy.24
  35.1 0.1 compare_reduce_fusion.1
  35.2 0.2 reduce_window_sum.17
  35.4 0.1 copy.26
  35.5 0.1 compare_reduce_fusion
  35.6 0.2 reduce_window_sum.18
  35.9 0.1 convert_element_type.97
  36.0 0.1 reshape.233.cross2
  36.1 0.1 convert_element_type.93
  36.2 0.1 constant_dynamic-slice_fusion.1
  36.3 0.2 copy.28
  36.5 0.1 broadcast_in_dim.40
  36.6 0.1 reshape.231.local2
  36.7 1.3 copy-done.1
  38.0 2.5 %adapter.1 = (bf16[2,10,96,512]{3,2,1,0:T(8,128)(2,1)S(1)}, bf16[64,5120]{1,0:T(8,128)(2,1)S(1)}, bf16[64,5120]{1,0:T(8,128)(2,1)S(1)}) custom-call(bf16[128,5120]{1,0:T(8,128)(2,1)S(1)} %bitcast.47, bf16[128,5120]{1,0:T(8,128)(2,1)S(1)} %bitcast.48, f32[96,1]{1,0:T(8,128)S(1)} %reshape.240.keep_ref, bf16[64,5120]{1,0:T(8,128)(2,1)S(1)} %bitcast.46, ...), custom_call_target="tpu_custom_call" | custom-call | flops 377487360 | bytes 10485760 | tf_op jit(solution)/shard_map/adapter/pallas_call | solution.py:198
  40.5 0.1 copy.32
  40.6 0.1 copy.33
  40.7 0.1 pad_maximum_fusion
  40.8 147.9 %route.1 = (bf16[96,5120]{1,0:T(8,128)(2,1)S(1)}, bf16[96,5120]{1,0:T(8,128)(2,1)S(1)}, f32[1,5120]{1,0:T(1,128)S(1)}, f32[1,5120]{1,0:T(1,128)S(1)}) custom-call(bf16[2,10,96,512]{3,2,1,0:T(8,128)(2,1)S(1)} %get-tuple-element.14.src, f32[1,48]{1,0:T(1,128)S(1)} %convert_element_type.90.local1, f32[4,64]{1,0:T(4,128)S(1)} %reshape.231.local2, ...), custom_call_target="tpu_custom_call" | custom-call | tf_op jit(solution)/shard_map/route/pallas_call | solution.py:588
  188.7 0.9 copy.40
  189.7 0.9 copy.41
  190.6 0.6 copy.42
  191.2 0.6 copy.43
  (26 shorter events, 0.4 us)
Async XLA Ops:
  34.5 2.2 %copy-start = (bf16[1,1,16,8,5120]{4,3,2,1,0:T(8,128)(2,1)S(1)}, bf16[1,1,16,8,5120]{4,3,2,1,0:T(8,128)(2,1)}, u32[]{:S(2)}) copy-start(bf16[1,1,16,8,5120]{4,3,2,1,0:T(8,128)(2,1)} %param.8) | copy-start | bytes 3932164
  34.5 2.2 %copy-start.2 = (bf16[1,5120]{1,0:T(2,128)(2,1)S(1)}, bf16[1,5120]{1,0:T(2,128)(2,1)}, u32[]{:S(2)}) copy-start(bf16[1,5120]{1,0:T(2,128)(2,1)} %gain_ref.1) | copy-start | bytes 30724
  36.7 1.3 copy-start.1
